TPU v7x, 256 devices: a whole 4x4x8 slice. The times are simulated.
256 devices in a mesh: chan: 16 (over x, z_hi, core), batch: 16 (over y, z_lo).
Axes of the slice: x: 4, y: 4, z: 8 (z_hi: 2, z_lo: 4; z = z_hi * 4 + z_lo), core: 2. Of those that a mesh axis runs over, the one named last changes fastest.
Arguments:
- fields: bfloat16 [16, 1536, 4096], P('batch', None, 'chan'), may hold values from -6 to 6
- norm1_gain: float32 [1536], replicated, may hold values from 0.5 to 1.5
- norm1_shift: float32 [1536], replicated, may hold values from -1.75 to 1.75
- spec_w1: float32 [2, 32, 48, 48], P(None, 'chan'), may hold values from -0.625 to 0.625
- spec_b1: float32 [2, 32, 48], P(None, 'chan'), may hold values from -1.75 to 1.75
- spec_w2: float32 [2, 32, 48, 48], P(None, 'chan'), may hold values from -0.625 to 0.625
- spec_b2: float32 [2, 32, 48], P(None, 'chan'), may hold values from -1.75 to 1.75
- norm2_gain: float32 [1536], replicated, may hold values from 0.5 to 1.5
- norm2_shift: float32 [1536], replicated, may hold values from -1.75 to 1.75
- w_in: bfloat16 [1536, 3072], P(None, 'batch'), may hold values from -0.15625 to 0.15625
- b_in: float32 [3072], replicated, may hold values from -1.75 to 1.75
- w_out: bfloat16 [3072, 1536], P('batch'), may hold values from -0.109375 to 0.109375
- b_out: float32 [1536], replicated, may hold values from -1.75 to 1.75
Outputs:
- mixed: bfloat16 [16, 1536, 4096], P('batch', None, 'chan')
All inputs are finite; a program needn't handle non-finite values.
Results may differ from a plain program's by a relative error of at most 0.008.
Values may be sent and summed in bfloat16 or wider, within the bound.
A program may use at most 128 MiB of HBM per device.

v0:
```python
import math

import jax
import jax.numpy as jnp
from jax import lax
from jax.sharding import PartitionSpec as P

BSIZE = 48
GRID = 16


highest = lax.Precision.HIGHEST
shrink_level = 0.2


def layer_norm(values, gain_vec, shift_vec):
    widened = values.astype(jnp.float32)
    center = widened - jnp.mean(widened, axis=1, keepdims=True)
    spread = jnp.mean(center * center, axis=1, keepdims=True)
    return (
        center * lax.rsqrt(spread + 1e-05) * gain_vec[None, :, None] + shift_vec[None, :, None]
    ).astype(jnp.bfloat16)


def dft_tables(length_grid):
    half_count = length_grid // 2 + 1
    position = jnp.arange(length_grid, dtype=jnp.int32)
    frequency = jnp.arange(half_count, dtype=jnp.int32)
    phase_index = (
        position[:, None, None, None] * position[None, None, :, None]
        + position[None, :, None, None] * frequency[None, None, None, :]
    ) % length_grid
    angle_grid = phase_index.astype(jnp.float32) * (2.0 * math.pi / length_grid)
    flat_size = length_grid * length_grid
    cos_plane = jnp.cos(angle_grid).reshape(flat_size, length_grid * half_count)
    sin_plane = jnp.sin(angle_grid).reshape(flat_size, length_grid * half_count)
    edge_mode = (frequency == 0) | (frequency == length_grid // 2)
    mode_weight = jnp.tile(jnp.where(edge_mode, 1.0, 2.0).astype(jnp.float32), length_grid)
    forward_plane = jnp.concatenate([cos_plane, -sin_plane], axis=1) / length_grid
    inverse_plane = (
        jnp.concatenate(
            [(cos_plane * mode_weight[None, :]).T, -(sin_plane * mode_weight[None, :]).T], axis=0
        )
        / length_grid
    )
    line_angle = (position[:, None] * position[None, :] % length_grid).astype(jnp.float32) * (
        2.0 * math.pi / length_grid
    )
    cos_line = jnp.cos(line_angle) / math.sqrt(length_grid)
    sin_line = jnp.sin(line_angle) / math.sqrt(length_grid)
    return (forward_plane, inverse_plane, cos_line, sin_line)


def along_line(table_mat, values):
    return jnp.einsum("ka,fcam->fckm", table_mat, values, precision=highest)


def block_mix(values, weight):
    return jnp.einsum("fbiam,bio->fboam", values, weight, precision=highest)


def with_bias(bias_vec):
    return bias_vec[None, :, :, None, None]


def shrink(values):
    return jnp.where(
        values > shrink_level,
        values - shrink_level,
        jnp.where(values < -shrink_level, values + shrink_level, jnp.zeros_like(values)),
    )


def spectral(channel_block, spec_w1, spec_b1, spec_w2, spec_b2):
    frames, channels, tokens_all = channel_block.shape
    mode_count = GRID * (GRID // 2 + 1)
    forward_plane, inverse_plane, cos_line, sin_line = dft_tables(GRID)
    plane_high = forward_plane.astype(jnp.bfloat16)
    plane_low = (forward_plane - plane_high.astype(jnp.float32)).astype(jnp.bfloat16)
    flat_rows = channel_block.reshape(frames * channels * GRID, GRID * GRID)
    plane_spec = jnp.dot(flat_rows, plane_high, preferred_element_type=jnp.float32) + jnp.dot(
        flat_rows, plane_low, preferred_element_type=jnp.float32
    )
    plane_spec = plane_spec.reshape(frames, channels, GRID, 2 * mode_count)
    plane_re = plane_spec[..., :mode_count]
    plane_im = plane_spec[..., mode_count:]
    spec_re = along_line(cos_line, plane_re) + along_line(sin_line, plane_im)
    spec_im = along_line(cos_line, plane_im) - along_line(sin_line, plane_re)
    block_count = channels // BSIZE
    block_shape = (frames, block_count, BSIZE, GRID, mode_count)
    spec_re = spec_re.reshape(block_shape)
    spec_im = spec_im.reshape(block_shape)
    mid_re = jax.nn.gelu(
        block_mix(spec_re, spec_w1[0]) - block_mix(spec_im, spec_w1[1]) + with_bias(spec_b1[0]),
        approximate=False,
    )
    mid_im = jax.nn.gelu(
        block_mix(spec_im, spec_w1[0]) + block_mix(spec_re, spec_w1[1]) + with_bias(spec_b1[1]),
        approximate=False,
    )
    out_re = shrink(
        block_mix(mid_re, spec_w2[0]) - block_mix(mid_im, spec_w2[1]) + with_bias(spec_b2[0])
    )
    out_im = shrink(
        block_mix(mid_im, spec_w2[0]) + block_mix(mid_re, spec_w2[1]) + with_bias(spec_b2[1])
    )
    out_re = out_re.reshape(frames, channels, GRID, mode_count)
    out_im = out_im.reshape(frames, channels, GRID, mode_count)
    back_re = along_line(cos_line, out_re) - along_line(sin_line, out_im)
    back_im = along_line(cos_line, out_im) + along_line(sin_line, out_re)
    joined = jnp.concatenate([back_re, back_im], axis=3).reshape(
        frames * channels * GRID, 2 * mode_count
    )
    spatial = jnp.dot(joined, inverse_plane, precision=highest).reshape(
        frames, channels, tokens_all
    )
    return (spatial + channel_block.astype(jnp.float32)).astype(jnp.bfloat16)


def on_device(
    fields,
    norm1_gain,
    norm1_shift,
    spec_w1,
    spec_b1,
    spec_w2,
    spec_b2,
    norm2_gain,
    norm2_shift,
    w_in,
    b_in,
    w_out,
    b_out,
):
    normed = layer_norm(fields, norm1_gain, norm1_shift)
    filtered_block = spectral(
        lax.all_to_all(normed, "chan", split_axis=1, concat_axis=2, tiled=True),
        spec_w1,
        spec_b1,
        spec_w2,
        spec_b2,
    )
    filtered = lax.all_to_all(filtered_block, "chan", split_axis=2, concat_axis=1, tiled=True)
    hidden_state = fields.astype(jnp.float32) + filtered.astype(jnp.float32)
    z_norm = layer_norm(hidden_state, norm2_gain, norm2_shift)
    token_rows = jnp.swapaxes(z_norm, 1, 2)
    pre_act = (
        jnp.einsum(
            "ftd,dk->ftk",
            token_rows,
            lax.all_gather(w_in, "batch", axis=1, tiled=True),
            preferred_element_type=jnp.float32,
        )
        + b_in
    )
    units = jax.nn.gelu(pre_act, approximate=False).astype(jnp.bfloat16)
    projected_rows = jnp.einsum(
        "ftk,kd->ftd",
        units,
        lax.all_gather(w_out, "batch", axis=0, tiled=True),
        preferred_element_type=jnp.float32,
    )
    projected = jnp.swapaxes(projected_rows, 1, 2)
    return (hidden_state + projected + b_out[None, :, None]).astype(jnp.bfloat16)


def solution(mesh):
    return jax.shard_map(
        on_device,
        mesh=mesh,
        in_specs=(
            P("batch", None, "chan"),
            P(),
            P(),
            P(None, "chan", None, None),
            P(None, "chan", None),
            P(None, "chan", None, None),
            P(None, "chan", None),
            P(),
            P(),
            P(None, "batch"),
            P(),
            P("batch", None),
            P(),
        ),
        out_specs=P("batch", None, "chan"),
        check_vma=False,
    )
```

profile of v0, /device:TPU:1, one launch (start us, length us, event | category | flops | bytes accessed | tf_op | source)
XLA Modules:
  0.0 488.8 jit_solution(7289557446443868913)
XLA Ops:
  11.1 8.2 %reduce.4 = bf16[1536,256]{1,0:T(8,128)(2,1)S(1)} reduce(bf16[1536,1,256]{2,1,0:T(2,128)(2,1)S(1)} %bitcast.294, bf16[]{:T(256)} %broadcast.566), dimensions={1}, to_apply=%bitcast.268.reduce_sub_computation | reduce | bytes 1572866
  20.3 12.4 %all-to-all-start = ((bf16[16,2,12288]{2,1,0:T(2,128)(2,1)}), bf16[16,2,12288]{2,1,0:T(2,128)(2,1)S(1)}, u32[]{:S(2)}, u32[]{:S(2)}) async-start(bf16[16,2,12288]{2,1,0:T(2,128)(2,1)} %reshape.497), calls=%async_computation | async-start | bytes 1572864 | tf_op jit(solution)/shard_map/all_to_all | solution.py:137
  35.0 27.2 %all-to-all-done = bf16[16,2,12288]{2,1,0:T(2,128)(2,1)S(1)} async-done(((bf16[16,2,12288]{2,1,0:T(2,128)(2,1)}), bf16[16,2,12288]{2,1,0:T(2,128)(2,1)S(1)}, u32[]{:S(2)}, u32[]{:S(2)}) %all-to-all-start) | async-done | bytes 786464 | tf_op jit(solution)/shard_map/all_to_all | solution.py:137
  66.0 2.1 copy.116
  68.2 2.3 fusion.251
  70.4 2.6 copy.147
  73.0 2.6 copy.148
  76.8 2.2 fusion.94
  79.0 3.6 copy.119
  85.0 2.4 copy.122
  87.4 3.7 fusion.89
  91.1 2.5 fusion.85
  93.7 5.8 %fusion.21 = f32[2,48,16,144]{3,1,2,0:T(8,128)S(1)} fusion(f32[2,16,144,48]{2,3,1,0:T(8,128)S(1)} %fusion.89, f32[2,48,16,144]{3,2,1,0:T(8,128)S(1)} %bitcast.301, f32[2,48]{1,0:T(2,128)S(1)} %get-tuple-element.13, f32[2,2,48,48]{3,2,1,0:T(8,128)S(1)} %copy-done.11), kind=kOutput, calls=%fused_computation.38 | convolution fusion | flops 142000128 | bytes 4080640 | tf_op jit(solution)/shard_map/fbiam,bio->fboam/dot_general | solution.py:59
  101.0 6.2 %fusion.23 = f32[2,48,16,144]{3,1,2,0:T(8,128)S(1)} fusion(f32[2,16,144,48]{2,3,1,0:T(8,128)S(1)} %fusion.85, f32[2,48,16,144]{3,2,1,0:T(8,128)S(1)} %bitcast.299, f32[2,48]{1,0:T(2,128)S(1)} %get-tuple-element.14, f32[2,2,48,48]{3,2,1,0:T(8,128)S(1)} %copy-done.11), kind=kOutput, calls=%fused_computation.40 | convolution fusion | flops 142000128 | bytes 4080640 | tf_op jit(solution)/shard_map/fbiam,bio->fboam/dot_general | solution.py:59
  109.1 2.1 copy.129
  111.2 2.6 copy.130
  113.8 2.9 fusion.127
  116.7 1.9 select_bitcast_fusion
  118.6 2.1 copy.131
  120.7 2.6 copy.132
  129.8 2.4 copy.135
  132.2 3.8 fusion.113
  139.1 5.0 %copy.137 = bf16[1,96,4096]{1,0,2:T(2,128)(2,1)S(1)} copy(bf16[1,96,4096]{2,1,0:T(8,128)(2,1)} %add_convert_fusion.1) | data formatting | bytes 1572864 | tf_op jit(solution)/shard_map/convert_element_type | solution.py:117
  144.1 23.4 %reduce.5 = bf16[4096,96]{1,0:T(8,128)(2,1)} reduce(bf16[4096,1,96]{2,1,0:T(2,128)(2,1)S(1)} %bitcast.288, bf16[]{:T(256)} %broadcast.566), dimensions={1}, to_apply=%bitcast.270.reduce_sub_computation | reduce | bytes 1572866
  167.5 3.3 reshape.499
  170.8 29.9 %all_to_all.24 = bf16[16,2,12288]{2,1,0:T(2,128)(2,1)} all-to-all(bf16[16,2,12288]{2,1,0:T(2,128)(2,1)S(1)} %reshape.499), channel_id=1, replica_groups=mesh['chan'=16,'batch'=16] {'chan'}, dimensions={0} | all-to-all | bytes 1572864 | tf_op jit(solution)/shard_map/all_to_all | solution.py:143
  200.7 4.5 reshape.500
  205.2 3.9 copy.138
  210.6 2.1 copy.139
  215.3 39.6 %all-gather.3.cloned.1.call-done = bf16[1536,3072]{0,1:T(8,128)(2,1)} async-done(((bf16[1536,192]{0,1:T(8,128)(2,1)}), bf16[1536,3072]{0,1:T(8,128)(2,1)}) %all-gather.3.cloned.1.call-update) | async-done | bytes 9437200 | tf_op jit(solution)/shard_map/all_gather | solution.py:151
  254.8 209.0 %all-gather.5.cloned.1.call-done = bf16[3072,1536]{1,0:T(8,128)(2,1)} async-done(((bf16[192,1536]{1,0:T(8,128)(2,1)}), bf16[3072,1536]{1,0:T(8,128)(2,1)}) %all-gather.5.cloned.1.call-update) | async-done | bytes 9437200 | tf_op jit(solution)/shard_map/all_gather | solution.py:160
  463.8 16.8 %fusion.12 = bf16[1,1536,256]{1,2,0:T(8,128)(2,1)S(1)} fusion(bf16[3072,1536]{1,0:T(8,128)(2,1)} %all-gather.5.cloned.1.call-done, bf16[1536,3072]{0,1:T(8,128)(2,1)} %all-gather.3.cloned.1.call-done, f32[3072]{0:T(1024)S(1)} %copy-done.16, f32[1536]{0:T(1024)S(1)} %copy-done.17, f32[1536]{0:T(1024)S(1)} %copy-done.18, f32[1536]{0:T(1024)S(1)} %copy-done.19, ...), kind=kOutput, calls=%fused_computation.24 | convolution fusion | flops 4888461312 | bytes 22052864 | tf_op jit(solution)/shard_map/ftk,kd->ftd/dot_general | solution.py:157
  (91 shorter events, 33.0 us)
Async XLA Ops:
  6.5 1.5 copy-start.6
  6.5 248.3 %all-gather.3.cloned.1.call-start = ((), (), s32[]{:S(2)}) async-start(), calls=%async_computation.2 | async-start | bytes 10027008 | tf_op jit(solution)/shard_map/all_gather | solution.py:151
  7.3 456.5 %all-gather.5.cloned.1.call-start = ((), (), s32[]{:S(2)}) async-start(), calls=%async_computation.3 | async-start | bytes 10027008 | tf_op jit(solution)/shard_map/all_gather | solution.py:160
  8.0 0.9 copy-start.12
  8.0 0.9 copy-start.13
  20.3 41.9 %all-to-all-start = ((bf16[16,2,12288]{2,1,0:T(2,128)(2,1)}), bf16[16,2,12288]{2,1,0:T(2,128)(2,1)S(1)}, u32[]{:S(2)}, u32[]{:S(2)}) async-start(bf16[16,2,12288]{2,1,0:T(2,128)(2,1)} %reshape.497), calls=%async_computation | async-start | bytes 1572864 | tf_op jit(solution)/shard_map/all_to_all | solution.py:137
  32.8 0.9 copy-start.14
  32.8 0.9 copy-start.15
  63.1 0.9 copy-start
  85.0 2.4 copy-start.2
  87.4 3.7 copy-start.5
  87.4 3.7 copy-start.11
  93.7 5.8 %copy-start.9 = (f32[2,2,48,48]{3,2,1,0:T(8,128)S(1)}, f32[2,2,48,48]{3,2,1,0:T(8,128)}, u32[]{:S(2)}) copy-start(f32[2,2,48,48]{3,2,1,0:T(8,128)} %param.18) | copy-start | bytes 110596
  99.5 1.5 copy-start.3
  107.2 1.9 copy-start.4
  113.8 2.9 copy-start.10
  129.8 2.4 copy-start.7
  129.8 2.5 copy-start.8
  136.1 1.6 copy-start.1
  214.8 249.0 %copy-start.16 = (f32[3072]{0:T(1024)S(1)}, f32[3072]{0:T(1024)}, u32[]{:S(2)}) copy-start(f32[3072]{0:T(1024)} %param.23) | copy-start | bytes 36868
  214.8 248.9 %copy-start.17 = (f32[1536]{0:T(1024)S(1)}, f32[1536]{0:T(1024)}, u32[]{:S(2)}) copy-start(f32[1536]{0:T(1024)} %param.25) | copy-start | bytes 18436
  214.8 248.9 %copy-start.18 = (f32[1536]{0:T(1024)S(1)}, f32[1536]{0:T(1024)}, u32[]{:S(2)}) copy-start(f32[1536]{0:T(1024)} %param.21) | copy-start | bytes 18436
  214.9 248.9 %copy-start.19 = (f32[1536]{0:T(1024)S(1)}, f32[1536]{0:T(1024)}, u32[]{:S(2)}) copy-start(f32[1536]{0:T(1024)} %param.20) | copy-start | bytes 18436
Sparse Core Ops, SparseCore 0:
  9.1 245.6 all-gather.2
  256.6 207.1 all-gather.4
where the time goes:
time: 495 us; the launch traced here: 489 us
  waiting for transfers between devices  277 us (56%)
  matrix products  59.7 us (12%)
  local copies, waits for them, and re-layouts  58 us (12%)
  other arithmetic  37.4 us (8%)
  blocking collectives  29.9 us (6%)
  between operations  14.2 us (3%)
  starting transfers between devices  12.5 us (3%)
    all_gather x1, waiting for transfers between devices, on_device(): lax.all_gather(w_out, 'batch', axis=0, tiled=True)  209 us
    all_gather x1, waiting for transfers between devices, on_device(): lax.all_gather(w_in, 'batch', axis=1, tiled=True)  39.6 us
    unnamed x3, other arithmetic  31.8 us
    all_to_all x1, blocking collectives, on_device(): lax.all_to_all(filtered_block, 'chan', split_axis=2, concat_axis=1, tiled...  29.9 us
    all_to_all x1, waiting for transfers between devices, on_device(): lax.all_to_all(normed, 'chan', split_axis=1, concat_axis=2, tiled=True)  27.2 us
    dot_general x8, matrix products, block_mix(): return jnp.einsum('fbiam,bio->fboam', values, weight, precision=highest)  26.4 us
    unnamed x50, local copies, waits for them, and re-layouts  17.7 us
    dot_general x1, matrix products, on_device(): jnp.einsum('ftk,kd->ftd', units, lax.all_gather(w_out, 'batch', axis=0, t...  16.8 us
  transfers between devices with their start and end apart: 3, of which 3 were waited for; matrix products, arithmetic and copies ran while one was open for 28% of the time, Pallas kernels for 0%

commit v1 on v0

v1 whole, which is shorter than its diff:
```python
import math

import jax
import jax.numpy as jnp
import numpy as np
from jax import lax
from jax.experimental import pallas as pl
from jax.experimental.pallas import tpu as pltpu
from jax.sharding import PartitionSpec as P

D = 1536
TOK = 256
CH = 96
HALF = 48
GRID = 16
MODES = 144
SHRINK = 0.2
MESH = pl.DeviceIdType.MESH
F32 = jnp.float32
BF16 = jnp.bfloat16


def plane_tables():
    pos = np.arange(GRID)
    freq = np.arange(GRID // 2 + 1)
    phase = (
        pos[:, None, None, None] * pos[None, None, :, None]
        + pos[None, :, None, None] * freq[None, None, None, :]
    ) % GRID
    angle = phase * (2.0 * math.pi / GRID)
    cos = np.cos(angle).reshape(TOK, MODES) / 64.0
    sin = np.sin(angle).reshape(TOK, MODES) / 64.0
    weight = np.tile(np.where((freq == 0) | (freq == GRID // 2), 1.0, 2.0), GRID)
    forward = np.concatenate([cos, -sin], axis=1).T
    inverse = np.zeros((512, TOK))
    inverse[:MODES] = (cos * weight).T
    inverse[256 : 256 + MODES] = -(sin * weight).T
    return jnp.asarray(forward, BF16), jnp.asarray(inverse, BF16)


def turned(value, step, sign):
    re, im = value
    step = step % 16
    if step == 0:
        return value
    if step == 8:
        return (-re, -im)
    if step == 4:
        return (-im, re) if sign > 0 else (im, -re)
    if step == 12:
        return (im, -re) if sign > 0 else (-im, re)
    c = math.cos(2.0 * math.pi * step / 16)
    s = sign * math.sin(2.0 * math.pi * step / 16)
    return (re * c - im * s, re * s + im * c)


def fft_list(values, sign):
    n = len(values)
    if n == 1:
        return values
    even = fft_list(values[0::2], sign)
    odd = fft_list(values[1::2], sign)
    out = [None] * n
    for k in range(n // 2):
        t = turned(odd[k], k * (16 // n), sign)
        e = even[k]
        out[k] = (e[0] + t[0], e[1] + t[1])
        out[k + n // 2] = (e[0] - t[0], e[1] - t[1])
    return out


def erf(v):
    x = jnp.clip(v, -3.832506856900711, 3.832506856900711)
    s = x * x
    p = -2.72614225801306e-10 * s + 2.77068142495902e-08
    p = p * s - 2.10102402082508e-06
    p = p * s - 5.69250639462346e-05
    p = p * s - 7.34990630326855e-04
    p = p * s - 2.95459980854025e-03
    p = p * s - 1.60960333262415e-02
    q = -1.45660718464996e-05 * s - 2.13374055278905e-04
    q = q * s - 1.68282697438203e-03
    q = q * s - 7.37332916720468e-03
    q = q * s - 1.42647390514189e-02
    return x * p / q


def gelu(v):
    half = 0.5 * v
    return half + half * erf(v * 0.7071067811865476)


def shrink(v):
    return v - jnp.clip(v, -SHRINK, SHRINK)


def dot_nt(a, b):
    return lax.dot_general(a, b, (((1,), (1,)), ((), ())), preferred_element_type=F32)


def dot(a, b):
    return jnp.dot(a, b, preferred_element_type=F32)


def loop(n, body):
    def step(i, carry):
        body(i)
        return carry

    lax.fori_loop(0, n, step, 0)


def kernel(
    fields, vecs, b_in, win, wout, mix1, mix2, bias1, bias2, fwd, inv, out,
    normed, recv1, plane, mid, back, fil, recv2, hid, zt, act, part, precv, own_t,
    win_all, wout_all,
    s1, r1, s2, r2, loc, zs, zr, ps, pr,
    b1s, b1r, b2s, b2r, b3s, b3r, a1s, a1r, a2s, a2r, a3s, a3r, a4s, a4r,
):
    chan = lax.axis_index("chan")
    batch = lax.axis_index("batch")
    x, zh, core = chan // 4, (chan // 2) % 2, chan % 2
    y, zl = batch // 4, batch % 4
    z = zh * 4 + zl

    def dev(xx, yy, zz, cc):
        xx, yy, zz = xx % 4, yy % 4, zz % 8
        return ((xx * 2 + zz // 4) * 2 + cc, yy * 4 + zz % 4)

    def remote(src, dst, ss, rs, to):
        return pltpu.make_async_remote_copy(
            src_ref=src, dst_ref=dst, send_sem=ss, recv_sem=rs, device_id=to, device_id_type=MESH
        )

    def peer(j, way):
        dz, dx, dc = j // 8, (j // 2) % 4, j % 2
        px, pz, pc = (x + way * dx + 4) % 4, (zh + dz) % 2, (core + dc) % 2
        return (px * 2 + pz) * 2 + pc

    zp, zm = dev(x, y, z + 1, core), dev(x, y, z + 7, core)
    zp2, zm2 = dev(x, y, z + 2, core), dev(x, y, z + 6, core)
    yp, ym, y2 = dev(x, y + 1, z, core), dev(x, y + 3, z, core), dev(x, y + 2, z, core)
    xp, xm = dev(x + 1, y, z, core), dev(x + 3, y, z, core)
    mate = dev(x, y, z, 1 - core)

    barrier = pltpu.get_barrier_semaphore()

    def greet(j, carry):
        pl.semaphore_signal(barrier, inc=1, device_id=(peer(j, 1), batch), device_id_type=MESH)
        return carry

    lax.fori_loop(1, 16, greet, 0)
    for to in (zp, zm, zp2, zm2, yp, ym, y2):
        pl.semaphore_signal(barrier, inc=1, device_id=to, device_id_type=MESH)

    offs = (0, 3, 1, 2)

    def slot(dy, k):
        return ((y + dy) % 4) * 4 + (zl + offs[k]) % 4

    own_slot = slot(0, 0)
    keep_in = pltpu.make_async_copy(win, win_all.at[own_slot], loc.at[0])
    keep_in.start()
    keep_out = pltpu.make_async_copy(
        wout.at[:, pl.ds(pl.multiple_of(x * 384, 128), 384)], wout_all.at[x, own_slot], loc.at[1]
    )
    keep_out.start()

    def rows(i):
        return pl.ds(pl.multiple_of(i * CH, CH), CH)

    def norm(load, gain_at, write):
        def add(i, acc):
            return acc + jnp.sum(load(i).reshape(CH // 8, 8, TOK), axis=0)

        total = lax.fori_loop(0, 16, add, jnp.zeros((8, TOK), F32))
        mean = jnp.sum(total, axis=0, keepdims=True) * (1.0 / D)

        def add_square(i, acc):
            c = load(i) - mean
            return acc + jnp.sum((c * c).reshape(CH // 8, 8, TOK), axis=0)

        total = lax.fori_loop(0, 16, add_square, jnp.zeros((8, TOK), F32))
        var = jnp.sum(total, axis=0, keepdims=True) * (1.0 / D)
        scale = lax.rsqrt(var + 1e-05)

        def finish(i):
            v = vecs[rows(i), :]
            c = load(i) - mean
            gain, shift = v[:, gain_at : gain_at + 1], v[:, gain_at + 1 : gain_at + 2]
            write(i, (c * scale * gain + shift).astype(BF16))

        loop(16, finish)

    def load_fields(i):
        return fields[rows(i), :].astype(F32)

    def write_normed(i, v):
        normed[rows(i), :] = v

    norm(load_fields, 0, write_normed)
    pl.semaphore_wait(barrier, 22)

    def to_block(j):
        return remote(
            normed.at[rows(peer(j, 1))], recv1.at[chan, pl.ds(0, CH)], s1.at[j], r1.at[j], (peer(j, 1), batch)
        )

    def from_plane(j):
        return remote(
            normed.at[rows(chan)], recv1.at[peer(j, -1), pl.ds(0, CH)], s1.at[j], r1.at[j], (peer(j, 1), batch)
        )

    loop(15, lambda i: to_block(15 - i).start())
    keep = pltpu.make_async_copy(normed.at[rows(chan)], recv1.at[chan, pl.ds(0, CH)], loc.at[2])
    keep.start()

    def b2(k, way):
        at = win_all.at[slot(0, k)]
        return remote(at, at, b2s.at[way, k], b2r.at[way, k], ym if way else yp)

    def b2_in(k, way):
        at = win_all.at[slot(1 if way else 3, k)]
        return remote(at, at, b2s.at[way, k], b2r.at[way, k], ym if way else yp)

    def b3(k):
        at = win_all.at[slot(3 if k < 2 else 1, k)]
        return remote(at, at, b3s.at[k], b3r.at[k], yp if k < 2 else ym)

    def b3_in(k):
        at = win_all.at[slot(2, k)]
        return remote(at, at, b3s.at[k], b3r.at[k], yp if k < 2 else ym)

    keep_in.wait()
    keep_out.wait()
    b2(0, 0).start()
    b2(0, 1).start()

    def b1(k, half, frm):
        to = {1: zp, 2: zm, 3: zm2 if half else zp2}[k]
        span = pl.ds(0, CH) if k < 3 else pl.ds(half * HALF, HALF)
        n = k + half
        at = win_all.at[slot(0, k if frm else 0), span]
        return remote(at, at, b1s.at[n], b1r.at[n], to)

    def a1(k, frm):
        at = wout_all.at[x, slot(0, k if frm else 0)]
        to = {1: zp, 2: zm, 3: dev(x, y, z + 2 + 4 * core, core)}[k]
        return remote(at, at, a1s.at[k], a1r.at[k], to)

    for k in (1, 2, 3):
        a1(k, False).start()
    for k, half in ((1, 0), (2, 0), (3, 0), (3, 1)):
        b1(k, half, False).start()

    group_offs = (0, 3, 1, 2)

    def group(q, dy):
        return wout_all.at[q, pl.ds(((y + dy) % 4) * 4, 4)]

    def a2(r, frm):
        to = {1: yp, 2: ym, 3: y2}[r]
        at = group(x, group_offs[r] if frm else 0)
        return remote(at, at, a2s.at[r], a2r.at[r], to)

    def a3(r, way, frm):
        q = (x + ((1 if way else 3) if frm else 0)) % 4
        at = group(q, group_offs[r])
        return remote(at, at, a3s.at[way, r], a3r.at[way, r], xm if way else xp)

    def a4(r, frm):
        q = (x + (2 if frm else (3 if r < 2 else 1))) % 4
        at = group(q, group_offs[r])
        return remote(at, at, a4s.at[r], a4r.at[r], xp if r < 2 else xm)

    def service_z():
        for k in (1, 2, 3):
            a1(k, True).wait_recv()
        for r in (1, 2, 3):
            a2(r, False).start()
        a3(0, 0, False).start()
        a3(0, 1, False).start()
        for k in (1, 2, 3):
            b1(k, 0, True).wait_recv()
            if k == 3:
                b1(k, 1, True).wait_recv()
            b2(k, 0).start()
            b2(k, 1).start()

    def service_y():
        for k in (0, 1):
            b2_in(k, 0).wait_recv()
            b3(k).start()
        for k in (2, 3):
            b2_in(k, 1).wait_recv()
            b3(k).start()
        for r in (1, 2, 3):
            a2(r, True).wait_recv()
            a3(r, 0, False).start()
            a3(r, 1, False).start()

    def service_x():
        for r in (0, 1):
            a3(r, 0, True).wait_recv()
            a4(r, False).start()
        for r in (2, 3):
            a3(r, 1, True).wait_recv()
            a4(r, False).start()

    def clear(a):
        recv1[a, pl.ds(CH, 32), :] = jnp.zeros((32, TOK), BF16)
        back[a, :, pl.ds(128, 128)] = jnp.zeros((2 * CH, 128), F32)

    loop(16, clear)

    keep.wait()
    loop(15, lambda i: from_plane(15 - i).wait_recv())

    def planes(p):
        both = recv1[pl.ds(2 * p, 2)].reshape(256, TOK)
        plane[p] = dot_nt(fwd[...], both)

    loop(8, planes)
    service_z()

    def lines(t):
        re_at = pl.ds(pl.multiple_of(t * 8, 8), 8)
        im_at = pl.ds(pl.multiple_of(MODES + t * 8, 8), 8)
        vals = []
        for a in range(16):
            lanes = pl.ds((a % 2) * 128, 128)
            vals.append((plane[a // 2, re_at, lanes], plane[a // 2, im_at, lanes]))
        for a, (re, im) in enumerate(fft_list(vals, -1)):
            lanes = pl.ds((a % 2) * 128, 128)
            plane[a // 2, re_at, lanes] = re
            plane[a // 2, im_at, lanes] = im

    loop(18, lines)

    def mix(p):
        v = plane[p].astype(BF16)
        lhs = jnp.concatenate(
            [
                jnp.concatenate([v[:MODES, :128], v[MODES:, :128]], axis=1),
                jnp.concatenate([v[:MODES, 128:], v[MODES:, 128:]], axis=1),
            ],
            axis=0,
        )
        mid[...] = gelu(dot(lhs, mix1[...]) + bias1[...]).astype(BF16)
        for half in range(2):
            res = dot_nt(mix2[...], mid[pl.ds(half * MODES, MODES), :]) + bias2[...]
            back[2 * p + half, :, pl.ds(0, MODES)] = shrink(res)

    loop(8, mix)

    def lines_back(t):
        re_at = pl.ds(pl.multiple_of((t // 2) * 8, 8), 8)
        im_at = pl.ds(pl.multiple_of(CH + (t // 2) * 8, 8), 8)
        lanes = pl.ds(pl.multiple_of((t % 2) * 128, 128), 128)
        vals = [(back[a, re_at, lanes], back[a, im_at, lanes]) for a in range(16)]
        for a, (re, im) in enumerate(fft_list(vals, 1)):
            back[a, re_at, lanes] = re
            back[a, im_at, lanes] = im

    loop(24, lines_back)

    def planes_back(p):
        lhs = [
            jnp.concatenate([back[2 * p + i, :CH, :], back[2 * p + i, CH:, :]], axis=1).astype(BF16)
            for i in range(2)
        ]
        res = dot(jnp.concatenate(lhs, axis=0), inv[...])
        for i in range(2):
            v = res[i * CH : (i + 1) * CH] + recv1[2 * p + i, pl.ds(0, CH), :].astype(F32)
            fil[2 * p + i] = v.astype(BF16)

    loop(8, planes_back)

    def to_plane(j):
        return remote(fil.at[peer(j, 1)], recv2.at[rows(chan)], s2.at[j], r2.at[j], (peer(j, 1), batch))

    def from_block(j):
        return remote(fil.at[chan], recv2.at[rows(peer(j, -1))], s2.at[j], r2.at[j], (peer(j, 1), batch))

    loop(15, lambda i: to_plane(15 - i).start())
    keep = pltpu.make_async_copy(fil.at[chan], recv2.at[rows(chan)], loc.at[3])
    keep.start()
    service_y()
    service_x()
    keep.wait()
    loop(15, lambda i: from_block(15 - i).wait_recv())

    def hidden(i):
        hid[rows(i), :] = load_fields(i) + recv2[rows(i), :].astype(F32)

    loop(16, hidden)

    def write_z(i, v):
        recv2[rows(i), :] = v

    def load_hidden(i):
        return hid[rows(i), :]

    norm(load_hidden, 2, write_z)

    eye = (
        lax.broadcasted_iota(jnp.int32, (TOK, TOK), 0) == lax.broadcasted_iota(jnp.int32, (TOK, TOK), 1)
    ).astype(F32).astype(BF16)

    def turn(i):
        at = pl.ds(pl.multiple_of(i * 256, 256), 256)
        zt[0, :, at] = dot_nt(eye, recv2[at, :]).astype(BF16)

    loop(6, turn)
    send_z = remote(zt.at[0], zt.at[1], zs, zr, mate)
    send_z.start()

    def units(g, t):
        s0 = g * 4
        w = win_all[pl.ds(s0, 4)].reshape(384, D)
        at = pl.ds(pl.multiple_of(g * 384, 128), 384)
        act[t, :, at] = gelu(dot_nt(zt[t], w) + b_in[:, at]).astype(BF16)

    for k in (0, 1, 2, 3):
        for way in (0, 1):
            if (way == 0) != (k < 2):
                b2_in(k, way).wait_recv()
    for k in range(4):
        b3_in(k).wait_recv()
    loop(4, lambda g: units(g, 0))
    send_z.wait_recv()
    loop(4, lambda g: units(g, 1))

    for r in range(4):
        a3(r, 0 if r >= 2 else 1, True).wait_recv()
    for r in range(4):
        a4(r, True).wait_recv()

    def project_mate(q):
        at = pl.ds(pl.multiple_of(q * 384, 128), 384)
        part[:, at] = dot(act[1], wout_all[q].reshape(D, 384)).astype(BF16)

    loop(4, project_mate)
    send_part = remote(part, precv, ps, pr, mate)
    send_part.start()

    def project_own(q):
        at = pl.ds(pl.multiple_of(q * 384, 128), 384)
        own_t[:, at] = dot(act[0], wout_all[q].reshape(D, 384))

    loop(4, project_own)
    send_part.wait_recv()

    def finish(i):
        at = pl.ds(pl.multiple_of(i * 128, 128), 128)
        total = (own_t[:, at] + precv[:, at].astype(F32)).T
        out[at, :] = (hid[at, :] + total + vecs[at, :][:, 4:5]).astype(BF16)

    loop(12, finish)

    loop(15, lambda i: to_block(15 - i).wait_send())
    loop(15, lambda i: to_plane(15 - i).wait_send())
    send_z.wait_send()
    send_part.wait_send()
    for k, half in ((1, 0), (2, 0), (3, 0), (3, 1)):
        b1(k, half, False).wait_send()
    for k in (1, 2, 3):
        a1(k, False).wait_send()
        a2(k, False).wait_send()
    for k in range(4):
        for way in range(2):
            b2(k, way).wait_send()
            a3(k, way, False).wait_send()
        b3(k).wait_send()
        a4(k, False).wait_send()


def blocks_matrix(w, b):
    def diag(m):
        zero = jnp.zeros((HALF, HALF), F32)
        top = jnp.concatenate([m[0], zero], axis=1)
        low = jnp.concatenate([zero, m[1]], axis=1)
        return jnp.concatenate([top, low], axis=0)

    re, im = diag(w[0]), diag(w[1])
    full = jnp.stack([jnp.stack([re, im]), jnp.stack([-im, re])])
    return full, b.reshape(2, CH)


def on_device(
    fields, norm1_gain, norm1_shift, spec_w1, spec_b1, spec_w2, spec_b2,
    norm2_gain, norm2_shift, w_in, b_in, w_out, b_out,
):
    core = lax.axis_index("chan") % 2
    forward, inverse = plane_tables()
    m1, c1 = blocks_matrix(spec_w1, spec_b1)
    m1 = jnp.pad(m1, ((0, 0), (0, 0), (0, 32), (0, 32))).transpose(0, 2, 1, 3).reshape(256, 256)
    c1 = jnp.pad(c1, ((0, 0), (0, 32))).reshape(1, 256)
    m2, c2 = blocks_matrix(spec_w2, spec_b2)
    m2 = jnp.pad(m2, ((0, 0), (0, 0), (0, 32), (0, 0))).transpose(1, 3, 0, 2).reshape(192, 256)
    c2 = c2.reshape(192, 1)
    vecs = jnp.stack([norm1_gain, norm1_shift, norm2_gain, norm2_shift, b_out], axis=1)
    win = lax.dynamic_slice(w_in, (0, core * CH), (D, CH)).T
    wout = lax.dynamic_slice(w_out, (core * CH, 0), (CH, D))
    units_bias = lax.dynamic_slice(b_in.reshape(16, 2, CH), (0, core, 0), (16, 1, CH)).reshape(1, D)
    vmem = pl.BlockSpec(memory_space=pltpu.VMEM)
    dma = pltpu.SemaphoreType.DMA
    res = pl.pallas_call(
        kernel,
        out_shape=jax.ShapeDtypeStruct((D, TOK), BF16),
        in_specs=[vmem] * 11,
        out_specs=vmem,
        scratch_shapes=[
            pltpu.VMEM((D, TOK), BF16),
            pltpu.VMEM((16, 128, TOK), BF16),
            pltpu.VMEM((8, 2 * MODES, 256), F32),
            pltpu.VMEM((2 * MODES, 256), BF16),
            pltpu.VMEM((16, 2 * CH, 256), F32),
            pltpu.VMEM((16, CH, TOK), BF16),
            pltpu.VMEM((D, TOK), BF16),
            pltpu.VMEM((D, TOK), F32),
            pltpu.VMEM((2, TOK, D), BF16),
            pltpu.VMEM((2, TOK, D), BF16),
            pltpu.VMEM((TOK, D), BF16),
            pltpu.VMEM((TOK, D), BF16),
            pltpu.VMEM((TOK, D), F32),
            pltpu.VMEM((16, CH, D), BF16),
            pltpu.VMEM((4, 16, CH, 384), BF16),
            dma((16,)), dma((16,)), dma((16,)), dma((16,)), dma((4,)),
            dma, dma, dma, dma,
            dma((5,)), dma((5,)), dma((2, 4)), dma((2, 4)), dma((4,)), dma((4,)),
            dma((4,)), dma((4,)), dma((4,)), dma((4,)), dma((2, 4)), dma((2, 4)), dma((4,)), dma((4,)),
        ],
        compiler_params=pltpu.CompilerParams(
            collective_id=0, has_side_effects=True, vmem_limit_bytes=56 * 2**20
        ),
        name="block",
    )(
        fields[0], vecs, units_bias, win, wout, m1.astype(BF16), m2.astype(BF16), c1, c2, forward, inverse
    )
    return res[None]


def solution(mesh):
    return jax.shard_map(
        on_device,
        mesh=mesh,
        in_specs=(
            P("batch", None, "chan"),
            P(),
            P(),
            P(None, "chan", None, None),
            P(None, "chan", None),
            P(None, "chan", None, None),
            P(None, "chan", None),
            P(),
            P(),
            P(None, "batch"),
            P(),
            P("batch", None),
            P(),
        ),
        out_specs=P("batch", None, "chan"),
        check_vma=False,
    )
```

time: 495 us -> 124 us (0.25)
  waiting for transfers between devices: 277 us -> 0 us
  Pallas kernels: 0 us -> 112 us
  matrix products: 59.7 us -> 0 us
  local copies, waits for them, and re-layouts: 58 us -> 10.4 us
  other arithmetic: 37.4 us -> 0.32 us
  blocking collectives: 29.9 us -> 0 us
  between operations: 14.2 us -> 0.21 us
  starting transfers between devices: 12.5 us -> 0 us
    all_gather x2 -> x0, waiting for transfers between devices: 249 us -> none  [the longest x1 209 us: on_device(): lax.all_gather(w_out, 'batch', axis=0, tiled=True)]
    pallas_call x0 -> x1, Pallas kernels: none -> 112 us  [on_device(): pl.pallas_call(kernel, out_shape=jax.ShapeDtypeStruct((D, TOK), BF16), in...]
    dot_general x20 -> x0, matrix products: 59.7 us -> none  [the longest x8 26.4 us: block_mix(): return jnp.einsum('fbiam,bio->fboam', values, weight, precision=highest)]
    unnamed x3 -> x0, other arithmetic: 31.8 us -> none
    all_to_all x1 -> x0, blocking collectives: 29.9 us -> none  [on_device(): lax.all_to_all(filtered_block, 'chan', split_axis=2, concat_axis=1, tiled...]
    all_to_all x1 -> x0, waiting for transfers between devices: 27.2 us -> none  [on_device(): lax.all_to_all(normed, 'chan', split_axis=1, concat_axis=2, tiled=True)]
    unnamed x50 -> x27, local copies, waits for them, and re-layouts: 17.7 us -> 4.87 us
    all_to_all x1 -> x0, starting transfers between devices: 12.4 us -> none  [on_device(): lax.all_to_all(normed, 'chan', split_axis=1, concat_axis=2, tiled=True)]
  transfers between devices with their start and end apart: 3 -> 0, of which waited for: 3 -> 0; matrix products, arithmetic and copies ran while one was open for 28% -> 0% of each run, Pallas kernels for 0% -> 0%
where the time goes in v1:
time: 124 us; the launch traced here: 123 us
  Pallas kernels  112 us (90%)
  local copies, waits for them, and re-layouts  10.4 us (8%)
    pallas_call x1, Pallas kernels, on_device(): pl.pallas_call(kernel, out_shape=jax.ShapeDtypeStruct((D, TOK), BF16), in...  112 us
    unnamed x27, local copies, waits for them, and re-layouts  4.87 us

profile of v1, /device:TPU:1, one launch (start us, length us, event | category | flops | bytes accessed | tf_op | source)
XLA Modules:
  0.0 122.6 jit_solution(1171689057841549632)
XLA Ops:
  0.0 0.7 copy-done.11
  0.7 0.1 reshape.92
  0.8 0.6 pad.24
  1.4 0.0 copy-start.9
  1.4 0.0 copy-start.4
  1.5 0.6 copy-done.6
  2.1 0.0 copy-done.7
  2.1 0.0 copy-done.8
  2.2 0.0 copy-done.4
  2.2 0.1 reshape.90
  2.3 0.0 copy-start.3
  2.3 0.7 reshape.91.b_in
  3.0 0.1 stack.81
  3.1 0.1 fusion.15
  3.2 0.1 copy-done.3
  3.2 0.1 fusion.16
  3.3 0.1 pad_convert_fusion.2
  3.4 0.1 pad_bitcast_fusion.2
  3.6 0.1 copy.26
  3.7 0.7 copy.34
  4.4 0.1 pad_convert_fusion
  4.5 0.1 pad_bitcast_fusion
  4.6 0.0 copy-start.10
  4.7 0.0 copy-start.1
  4.7 0.1 copy.27
  4.8 0.6 copy.35
  5.4 0.8 reshape_reshape.4.bias2
  6.2 0.7 dynamic-slice_bitcast_fusion.win
  6.9 0.7 constant_dynamic-slice_fusion.wout
  7.7 1.2 copy.28.vecs
  8.8 111.7 %block.1 = bf16[1536,256]{1,0:T(8,128)(2,1)} custom-call(bf16[1536,256]{1,0:T(8,128)(2,1)} %bitcast.60, f32[1536,5]{1,0:T(8,128)} %copy.28.vecs, f32[1,1536]{1,0:T(1,128)} %reshape.91.b_in, bf16[96,1536]{1,0:T(8,128)(2,1)} %dynamic-slice_bitcast_fusion.win, bf16[96,1536]{1,0:T(8,128)(2,1)} %constant_dynamic-slice_fusion.wout, bf16[256,256]{1,0:T(8,128)(2,1)} %bitcast.61, ...), custom_call_target="tpu_custom_call" | custom-call | tf_op jit(solution)/shard_map/block/pallas_call | solution.py:508
  120.6 2.1 %copy.37 = bf16[1,1536,256]{2,1,0:T(8,128)(2,1)} copy(bf16[1,1536,256]{2,1,0:T(8,128)(2,1)} %bitcast.59) | data formatting | bytes 1572864
  (31 shorter events, 0.3 us)
Async XLA Ops:
  0.0 6.2 %copy-start = (bf16[1536,192]{0,1:T(8,128)(2,1)S(1)}, bf16[1536,192]{0,1:T(8,128)(2,1)}, u32[]{:S(2)}) copy-start(bf16[1536,192]{0,1:T(8,128)(2,1)} %param.24) | copy-start | bytes 1769476
  0.0 0.7 copy-start.11
  0.0 1.4 %copy-start.5 = (f32[1536]{0:T(1024)S(1)}, f32[1536]{0:T(1024)}, u32[]{:S(2)}) copy-start(f32[1536]{0:T(1024)} %param.16) | copy-start | bytes 18436
  1.4 0.7 copy-start.6
  1.4 0.7 copy-start.7
  1.4 0.7 copy-start.8
  1.4 0.7 copy-start.9
  1.4 0.8 copy-start.4
  2.1 1.0 copy-start.2
  2.3 0.9 copy-start.3
  4.6 0.8 copy-start.10
  4.7 2.3 %copy-start.1 = (bf16[192,1536]{1,0:T(8,128)(2,1)S(1)}, bf16[192,1536]{1,0:T(8,128)(2,1)}, u32[]{:S(2)}) copy-start(bf16[192,1536]{1,0:T(8,128)(2,1)} %param.26) | copy-start | bytes 1769476

commit v2 on v1

--- a/solution.py
+++ b/solution.py
@@ -113,9 +113,9 @@
 def kernel(
     fields, vecs, b_in, win, wout, mix1, mix2, bias1, bias2, fwd, inv, out,
     normed, recv1, plane, mid, back, fil, recv2, hid, zt, act, part, precv, own_t,
-    win_all, wout_all,
+    w_all,
     s1, r1, s2, r2, loc, zs, zr, ps, pr,
-    b1s, b1r, b2s, b2r, b3s, b3r, a1s, a1r, a2s, a2r, a3s, a3r, a4s, a4r,
+    zws, zwr, xs, xr, ys, yr, y2s, y2r, ays, ayr, axs, axr, ax2s, ax2r,
 ):
     chan = lax.axis_index("chan")
     batch = lax.axis_index("batch")
@@ -140,7 +140,7 @@
     zp, zm = dev(x, y, z + 1, core), dev(x, y, z + 7, core)
     zp2, zm2 = dev(x, y, z + 2, core), dev(x, y, z + 6, core)
     yp, ym, y2 = dev(x, y + 1, z, core), dev(x, y + 3, z, core), dev(x, y + 2, z, core)
-    xp, xm = dev(x + 1, y, z, core), dev(x + 3, y, z, core)
+    xp, xm, x2 = dev(x + 1, y, z, core), dev(x + 3, y, z, core), dev(x + 2, y, z, core)
     mate = dev(x, y, z, 1 - core)
 
     barrier = pltpu.get_barrier_semaphore()
@@ -159,12 +159,24 @@
         return ((y + dy) % 4) * 4 + (zl + offs[k]) % 4
 
     own_slot = slot(0, 0)
-    keep_in = pltpu.make_async_copy(win, win_all.at[own_slot], loc.at[0])
-    keep_in.start()
-    keep_out = pltpu.make_async_copy(
-        wout.at[:, pl.ds(pl.multiple_of(x * 384, 128), 384)], wout_all.at[x, own_slot], loc.at[1]
+    mine = pl.ds(pl.multiple_of(core * CH, CH), CH)
+    keeps = []
+    for q in range(4):
+        for n, (src, at, size, to) in enumerate(
+            ((win, 384 * q, 384, 0), (wout, 1024 + 128 * q, 128, 384))
+        ):
+            keeps.append(
+                pltpu.make_async_copy(
+                    src.at[mine, pl.ds(at, size)], w_all.at[q, own_slot, :, pl.ds(to, size)], loc.at[q, n]
+                )
+            )
+    keeps.append(
+        pltpu.make_async_copy(
+            wout.at[mine, pl.ds(pl.multiple_of(256 * x, 128), 256)], w_all.at[x, own_slot, :, pl.ds(512, 256)], loc.at[2, 3]
+        )
     )
-    keep_out.start()
+    for copy in keeps:
+        copy.start()
 
     def rows(i):
         return pl.ds(pl.multiple_of(i * CH, CH), CH)
@@ -198,8 +210,10 @@
     def write_normed(i, v):
         normed[rows(i), :] = v
 
-    norm(load_fields, 0, write_normed)
-    pl.semaphore_wait(barrier, 22)
+    with jax.named_scope("norm1"):
+        norm(load_fields, 0, write_normed)
+    with jax.named_scope("greet_wait"):
+        pl.semaphore_wait(barrier, 22)
 
     def to_block(j):
         return remote(
@@ -211,117 +225,124 @@
             normed.at[rows(chan)], recv1.at[peer(j, -1), pl.ds(0, CH)], s1.at[j], r1.at[j], (peer(j, 1), batch)
         )
 
-    loop(15, lambda i: to_block(15 - i).start())
-    keep = pltpu.make_async_copy(normed.at[rows(chan)], recv1.at[chan, pl.ds(0, CH)], loc.at[2])
+    first, last = pl.ds(0, 512), pl.ds(512, 256)
+
+    def z_move(k, came):
+        at = w_all.at[x, slot(0, k if came else 0)]
+        to = {1: zp, 2: zm, 3: dev(x, y, z + 2 + 4 * core, core)}[k]
+        return remote(at, at, zws.at[k], zwr.at[k], to)
+
+    def x_move(k, way, came):
+        at = w_all.at[(x + ((3, 1, 2)[way] if came else 0)) % 4, slot(0, k), :, first]
+        return remote(at, at, xs.at[way, k], xr.at[way, k], (xp, xm, x2)[way])
+
+    def y_move(k, way, came):
+        at = w_all.at[:, slot((3, 1)[way] if came else 0, k), :, first]
+        return remote(at, at, ys.at[way, k], yr.at[way, k], (yp, ym)[way])
+
+    def y_pass(k, came):
+        at = w_all.at[:, slot(2 if came else (3 if k < 2 else 1), k), :, first]
+        return remote(at, at, y2s.at[k], y2r.at[k], yp if k < 2 else ym)
+
+    def group(q, dy):
+        return w_all.at[q, pl.ds(((y + dy) % 4) * 4, 4), :, last]
+
+    def ay(r, came):
+        at = group(x, offs[r] if came else 0)
+        return remote(at, at, ays.at[r], ayr.at[r], {1: yp, 2: ym, 3: y2}[r])
+
+    def ax(r, way, came):
+        at = group((x + ((3, 1)[way] if came else 0)) % 4, offs[r])
+        return remote(at, at, axs.at[way, r], axr.at[way, r], (xp, xm)[way])
+
+    def ax_pass(r, came):
+        at = group((x + (2 if came else (3 if r < 2 else 1))) % 4, offs[r])
+        return remote(at, at, ax2s.at[r], ax2r.at[r], xp if r < 2 else xm)
+
+    for copy in keeps:
+        copy.wait()
+    for k in (1, 2, 3):
+        z_move(k, False).start()
+    with jax.named_scope("blocks_send"):
+        loop(15, lambda i: to_block(15 - i).start())
+    keep = pltpu.make_async_copy(normed.at[rows(chan)], recv1.at[chan, pl.ds(0, CH)], loc.at[0, 3])
     keep.start()
 
-    def b2(k, way):
-        at = win_all.at[slot(0, k)]
-        return remote(at, at, b2s.at[way, k], b2r.at[way, k], ym if way else yp)
-
-    def b2_in(k, way):
-        at = win_all.at[slot(1 if way else 3, k)]
-        return remote(at, at, b2s.at[way, k], b2r.at[way, k], ym if way else yp)
-
-    def b3(k):
-        at = win_all.at[slot(3 if k < 2 else 1, k)]
-        return remote(at, at, b3s.at[k], b3r.at[k], yp if k < 2 else ym)
-
-    def b3_in(k):
-        at = win_all.at[slot(2, k)]
-        return remote(at, at, b3s.at[k], b3r.at[k], yp if k < 2 else ym)
-
-    keep_in.wait()
-    keep_out.wait()
-    b2(0, 0).start()
-    b2(0, 1).start()
-
-    def b1(k, half, frm):
-        to = {1: zp, 2: zm, 3: zm2 if half else zp2}[k]
-        span = pl.ds(0, CH) if k < 3 else pl.ds(half * HALF, HALF)
-        n = k + half
-        at = win_all.at[slot(0, k if frm else 0), span]
-        return remote(at, at, b1s.at[n], b1r.at[n], to)
-
-    def a1(k, frm):
-        at = wout_all.at[x, slot(0, k if frm else 0)]
-        to = {1: zp, 2: zm, 3: dev(x, y, z + 2 + 4 * core, core)}[k]
-        return remote(at, at, a1s.at[k], a1r.at[k], to)
-
-    for k in (1, 2, 3):
-        a1(k, False).start()
-    for k, half in ((1, 0), (2, 0), (3, 0), (3, 1)):
-        b1(k, half, False).start()
-
-    group_offs = (0, 3, 1, 2)
-
-    def group(q, dy):
-        return wout_all.at[q, pl.ds(((y + dy) % 4) * 4, 4)]
-
-    def a2(r, frm):
-        to = {1: yp, 2: ym, 3: y2}[r]
-        at = group(x, group_offs[r] if frm else 0)
-        return remote(at, at, a2s.at[r], a2r.at[r], to)
-
-    def a3(r, way, frm):
-        q = (x + ((1 if way else 3) if frm else 0)) % 4
-        at = group(q, group_offs[r])
-        return remote(at, at, a3s.at[way, r], a3r.at[way, r], xm if way else xp)
-
-    def a4(r, frm):
-        q = (x + (2 if frm else (3 if r < 2 else 1))) % 4
-        at = group(q, group_offs[r])
-        return remote(at, at, a4s.at[r], a4r.at[r], xp if r < 2 else xm)
+    def start_y(k):
+        y_move(k, 0, False).start()
+        y_move(k, 1, False).start()
+
+    start_y(0)
 
     def service_z():
         for k in (1, 2, 3):
-            a1(k, True).wait_recv()
+            z_move(k, True).wait_recv()
+            for way in range(3):
+                x_move(k, way, False).start()
         for r in (1, 2, 3):
-            a2(r, False).start()
-        a3(0, 0, False).start()
-        a3(0, 1, False).start()
+            ay(r, False).start()
+        ax(0, 0, False).start()
+        ax(0, 1, False).start()
+
+    def service_y0():
+        y_move(0, 0, True).wait_recv()
+        y_pass(0, False).start()
+
+    def service_x():
         for k in (1, 2, 3):
-            b1(k, 0, True).wait_recv()
-            if k == 3:
-                b1(k, 1, True).wait_recv()
-            b2(k, 0).start()
-            b2(k, 1).start()
-
-    def service_y():
-        for k in (0, 1):
-            b2_in(k, 0).wait_recv()
-            b3(k).start()
+            for way in range(3):
+                x_move(k, way, True).wait_recv()
+            start_y(k)
+
+    def service_a():
+        for r in (1, 2, 3):
+            ay(r, True).wait_recv()
+            ax(r, 0, False).start()
+            ax(r, 1, False).start()
+
+    def service_y1():
+        y_move(1, 0, True).wait_recv()
+        y_pass(1, False).start()
+
+    def service_y2():
         for k in (2, 3):
-            b2_in(k, 1).wait_recv()
-            b3(k).start()
-        for r in (1, 2, 3):
-            a2(r, True).wait_recv()
-            a3(r, 0, False).start()
-            a3(r, 1, False).start()
-
-    def service_x():
+            y_move(k, 1, True).wait_recv()
+            y_pass(k, False).start()
+
+    def service_ax():
         for r in (0, 1):
-            a3(r, 0, True).wait_recv()
-            a4(r, False).start()
+            ax(r, 0, True).wait_recv()
+            ax_pass(r, False).start()
         for r in (2, 3):
-            a3(r, 1, True).wait_recv()
-            a4(r, False).start()
-
+            ax(r, 1, True).wait_recv()
+            ax_pass(r, False).start()
+
+    with jax.named_scope("service_z"):
+        service_z()
+    with jax.named_scope("service_y0"):
+        service_y0()
     def clear(a):
         recv1[a, pl.ds(CH, 32), :] = jnp.zeros((32, TOK), BF16)
         back[a, :, pl.ds(128, 128)] = jnp.zeros((2 * CH, 128), F32)
 
-    loop(16, clear)
+    with jax.named_scope("clear"):
+        loop(16, clear)
 
     keep.wait()
-    loop(15, lambda i: from_plane(15 - i).wait_recv())
+    with jax.named_scope("service_x"):
+        service_x()
+    with jax.named_scope("service_a"):
+        service_a()
+    with jax.named_scope("blocks_wait"):
+        loop(15, lambda i: from_plane(15 - i).wait_recv())
 
     def planes(p):
         both = recv1[pl.ds(2 * p, 2)].reshape(256, TOK)
         plane[p] = dot_nt(fwd[...], both)
 
-    loop(8, planes)
-    service_z()
+    with jax.named_scope("planes"):
+        loop(8, planes)
+
 
     def lines(t):
         re_at = pl.ds(pl.multiple_of(t * 8, 8), 8)
@@ -335,7 +356,8 @@
             plane[a // 2, re_at, lanes] = re
             plane[a // 2, im_at, lanes] = im
 
-    loop(18, lines)
+    with jax.named_scope("lines"):
+        loop(18, lines)
 
     def mix(p):
         v = plane[p].astype(BF16)
@@ -351,7 +373,8 @@
             res = dot_nt(mix2[...], mid[pl.ds(half * MODES, MODES), :]) + bias2[...]
             back[2 * p + half, :, pl.ds(0, MODES)] = shrink(res)
 
-    loop(8, mix)
+    with jax.named_scope("mix"):
+        loop(8, mix)
 
     def lines_back(t):
         re_at = pl.ds(pl.multiple_of((t // 2) * 8, 8), 8)
@@ -362,7 +385,8 @@
             back[a, re_at, lanes] = re
             back[a, im_at, lanes] = im
 
-    loop(24, lines_back)
+    with jax.named_scope("lines_back"):
+        loop(24, lines_back)
 
     def planes_back(p):
         lhs = [
@@ -374,7 +398,8 @@
             v = res[i * CH : (i + 1) * CH] + recv1[2 * p + i, pl.ds(0, CH), :].astype(F32)
             fil[2 * p + i] = v.astype(BF16)
 
-    loop(8, planes_back)
+    with jax.named_scope("planes_back"):
+        loop(8, planes_back)
 
     def to_plane(j):
         return remote(fil.at[peer(j, 1)], recv2.at[rows(chan)], s2.at[j], r2.at[j], (peer(j, 1), batch))
@@ -383,17 +408,23 @@
         return remote(fil.at[chan], recv2.at[rows(peer(j, -1))], s2.at[j], r2.at[j], (peer(j, 1), batch))
 
     loop(15, lambda i: to_plane(15 - i).start())
-    keep = pltpu.make_async_copy(fil.at[chan], recv2.at[rows(chan)], loc.at[3])
+    keep = pltpu.make_async_copy(fil.at[chan], recv2.at[rows(chan)], loc.at[1, 3])
     keep.start()
-    service_y()
-    service_x()
+    with jax.named_scope("service_y1"):
+        service_y1()
+    with jax.named_scope("service_ax"):
+        service_ax()
+    with jax.named_scope("service_y2"):
+        service_y2()
     keep.wait()
-    loop(15, lambda i: from_block(15 - i).wait_recv())
+    with jax.named_scope("filtered_wait"):
+        loop(15, lambda i: from_block(15 - i).wait_recv())
 
     def hidden(i):
         hid[rows(i), :] = load_fields(i) + recv2[rows(i), :].astype(F32)
 
-    loop(16, hidden)
+    with jax.named_scope("hidden"):
+        loop(16, hidden)
 
     def write_z(i, v):
         recv2[rows(i), :] = v
@@ -401,7 +432,8 @@
     def load_hidden(i):
         return hid[rows(i), :]
 
-    norm(load_hidden, 2, write_z)
+    with jax.named_scope("norm2"):
+        norm(load_hidden, 2, write_z)
 
     eye = (
         lax.broadcasted_iota(jnp.int32, (TOK, TOK), 0) == lax.broadcasted_iota(jnp.int32, (TOK, TOK), 1)
@@ -411,68 +443,101 @@
         at = pl.ds(pl.multiple_of(i * 256, 256), 256)
         zt[0, :, at] = dot_nt(eye, recv2[at, :]).astype(BF16)
 
-    loop(6, turn)
+    with jax.named_scope("turn"):
+        loop(6, turn)
     send_z = remote(zt.at[0], zt.at[1], zs, zr, mate)
     send_z.start()
 
-    def units(g, t):
-        s0 = g * 4
-        w = win_all[pl.ds(s0, 4)].reshape(384, D)
-        at = pl.ds(pl.multiple_of(g * 384, 128), 384)
-        act[t, :, at] = gelu(dot_nt(zt[t], w) + b_in[:, at]).astype(BF16)
-
-    for k in (0, 1, 2, 3):
-        for way in (0, 1):
-            if (way == 0) != (k < 2):
-                b2_in(k, way).wait_recv()
-    for k in range(4):
-        b3_in(k).wait_recv()
-    loop(4, lambda g: units(g, 0))
-    send_z.wait_recv()
-    loop(4, lambda g: units(g, 1))
-
-    for r in range(4):
-        a3(r, 0 if r >= 2 else 1, True).wait_recv()
-    for r in range(4):
-        a4(r, True).wait_recv()
-
-    def project_mate(q):
-        at = pl.ds(pl.multiple_of(q * 384, 128), 384)
-        part[:, at] = dot(act[1], wout_all[q].reshape(D, 384)).astype(BF16)
-
-    loop(4, project_mate)
+    def units(i, t):
+        g = [(y + offs[2 * i + n]) % 4 for n in range(2)]
+        w = jnp.concatenate(
+            [
+                jnp.concatenate([w_all[q, pl.ds(g[n] * 4, 4), :, :384].reshape(384, 384) for q in range(4)], axis=1)
+                for n in range(2)
+            ],
+            axis=0,
+        )
+        res = dot_nt(zt[t], w)
+        for n in range(2):
+            at = pl.ds(pl.multiple_of(g[n] * 384, 128), 384)
+            act[t, :, at] = gelu(res[:, n * 384 : (n + 1) * 384] + b_in[:, at]).astype(BF16)
+
+    with jax.named_scope("win_wait_a"):
+        for k in (2, 3):
+            y_move(k, 0, True).wait_recv()
+    with jax.named_scope("units_own_a"):
+        units(0, 0)
+    with jax.named_scope("z_wait"):
+        send_z.wait_recv()
+    with jax.named_scope("units_mate_a"):
+        units(0, 1)
+    with jax.named_scope("win_wait_b"):
+        for k in (0, 1):
+            y_move(k, 1, True).wait_recv()
+        for k in range(4):
+            y_pass(k, True).wait_recv()
+    with jax.named_scope("units_mate_b"):
+        units(1, 1)
+    with jax.named_scope("units_own_b"):
+        units(1, 0)
+    with jax.named_scope("wout_wait"):
+        for r in range(4):
+            ax(r, 0 if r >= 2 else 1, True).wait_recv()
+        for r in range(4):
+            ax_pass(r, True).wait_recv()
+
+    def project(t, write):
+        def one(q):
+            write(
+                pl.ds(pl.multiple_of(q * 256, 128), 256), dot(act[t], w_all[q, :, :, 512:].reshape(D, 256))
+            )
+
+        def two(i):
+            w = jnp.concatenate([w_all[2 * i + n, :, :, 384:512].reshape(D, 128) for n in range(2)], axis=1)
+            write(pl.ds(pl.multiple_of(1024 + i * 256, 128), 256), dot(act[t], w))
+
+        loop(2, two)
+        loop(4, one)
+
+    def write_part(at, v):
+        part[:, at] = v.astype(BF16)
+
+    def write_own(at, v):
+        own_t[:, at] = v
+
+    with jax.named_scope("project_mate"):
+        project(1, write_part)
     send_part = remote(part, precv, ps, pr, mate)
     send_part.start()
 
-    def project_own(q):
-        at = pl.ds(pl.multiple_of(q * 384, 128), 384)
-        own_t[:, at] = dot(act[0], wout_all[q].reshape(D, 384))
-
-    loop(4, project_own)
-    send_part.wait_recv()
+    with jax.named_scope("project_own"):
+        project(0, write_own)
+    with jax.named_scope("part_wait"):
+        send_part.wait_recv()
 
     def finish(i):
         at = pl.ds(pl.multiple_of(i * 128, 128), 128)
         total = (own_t[:, at] + precv[:, at].astype(F32)).T
         out[at, :] = (hid[at, :] + total + vecs[at, :][:, 4:5]).astype(BF16)
 
-    loop(12, finish)
+    with jax.named_scope("finish"):
+        loop(12, finish)
 
     loop(15, lambda i: to_block(15 - i).wait_send())
     loop(15, lambda i: to_plane(15 - i).wait_send())
     send_z.wait_send()
     send_part.wait_send()
-    for k, half in ((1, 0), (2, 0), (3, 0), (3, 1)):
-        b1(k, half, False).wait_send()
-    for k in (1, 2, 3):
-        a1(k, False).wait_send()
-        a2(k, False).wait_send()
     for k in range(4):
+        if k:
+            z_move(k, False).wait_send()
+            ay(k, False).wait_send()
+            for way in range(3):
+                x_move(k, way, False).wait_send()
         for way in range(2):
-            b2(k, way).wait_send()
-            a3(k, way, False).wait_send()
-        b3(k).wait_send()
-        a4(k, False).wait_send()
+            y_move(k, way, False).wait_send()
+            ax(k, way, False).wait_send()
+        y_pass(k, False).wait_send()
+        ax_pass(k, False).wait_send()
 
 
 def blocks_matrix(w, b):
@@ -500,15 +565,13 @@
     m2 = jnp.pad(m2, ((0, 0), (0, 0), (0, 32), (0, 0))).transpose(1, 3, 0, 2).reshape(192, 256)
     c2 = c2.reshape(192, 1)
     vecs = jnp.stack([norm1_gain, norm1_shift, norm2_gain, norm2_shift, b_out], axis=1)
-    win = lax.dynamic_slice(w_in, (0, core * CH), (D, CH)).T
-    wout = lax.dynamic_slice(w_out, (core * CH, 0), (CH, D))
     units_bias = lax.dynamic_slice(b_in.reshape(16, 2, CH), (0, core, 0), (16, 1, CH)).reshape(1, D)
     vmem = pl.BlockSpec(memory_space=pltpu.VMEM)
     dma = pltpu.SemaphoreType.DMA
     res = pl.pallas_call(
         kernel,
         out_shape=jax.ShapeDtypeStruct((D, TOK), BF16),
-        in_specs=[vmem] * 11,
+        in_specs=[vmem] * 3 + [pl.BlockSpec(memory_space=pl.ANY)] * 2 + [vmem] * 6,
         out_specs=vmem,
         scratch_shapes=[
             pltpu.VMEM((D, TOK), BF16),
@@ -524,19 +587,18 @@
             pltpu.VMEM((TOK, D), BF16),
             pltpu.VMEM((TOK, D), BF16),
             pltpu.VMEM((TOK, D), F32),
-            pltpu.VMEM((16, CH, D), BF16),
-            pltpu.VMEM((4, 16, CH, 384), BF16),
-            dma((16,)), dma((16,)), dma((16,)), dma((16,)), dma((4,)),
+            pltpu.VMEM((4, 16, CH, 768), BF16),
+            dma((16,)), dma((16,)), dma((16,)), dma((16,)), dma((4, 4)),
             dma, dma, dma, dma,
-            dma((5,)), dma((5,)), dma((2, 4)), dma((2, 4)), dma((4,)), dma((4,)),
-            dma((4,)), dma((4,)), dma((4,)), dma((4,)), dma((2, 4)), dma((2, 4)), dma((4,)), dma((4,)),
+            dma((4,)), dma((4,)), dma((3, 4)), dma((3, 4)), dma((2, 4)), dma((2, 4)), dma((4,)), dma((4,)),
+            dma((4,)), dma((4,)), dma((2, 4)), dma((2, 4)), dma((4,)), dma((4,)),
         ],
         compiler_params=pltpu.CompilerParams(
             collective_id=0, has_side_effects=True, vmem_limit_bytes=56 * 2**20
         ),
         name="block",
     )(
-        fields[0], vecs, units_bias, win, wout, m1.astype(BF16), m2.astype(BF16), c1, c2, forward, inverse
+        fields[0], vecs, units_bias, w_in.T, w_out, m1.astype(BF16), m2.astype(BF16), c1, c2, forward, inverse
     )
     return res[None]
 

time: 124 us -> 98.3 us (0.79)
  Pallas kernels: 112 us -> 87.5 us
  local copies, waits for them, and re-layouts: 10.4 us -> 8.89 us
    pallas_call x1, Pallas kernels: 112 us -> 87.5 us  [on_device(): pl.pallas_call(kernel, out_shape=jax.ShapeDtypeStruct((D, TOK), BF16), in...]
    unnamed x27 -> x23, local copies, waits for them, and re-layouts: 4.87 us -> 4.83 us
where the time goes in v2:
time: 98.3 us; the launch traced here: 96.9 us
  Pallas kernels  87.5 us (89%)
  local copies, waits for them, and re-layouts  8.89 us (9%)
    pallas_call x1, Pallas kernels, on_device(): pl.pallas_call(kernel, out_shape=jax.ShapeDtypeStruct((D, TOK), BF16), in...  87.5 us
    unnamed x23, local copies, waits for them, and re-layouts  4.83 us

profile of v2, /device:TPU:1, one launch (start us, length us, event | category | flops | bytes accessed | tf_op | source)
XLA Modules:
  0.0 96.9 jit_solution(16005223417882696872)
XLA Ops:
  0.0 0.7 copy-done.9
  0.7 0.1 reshape.92
  0.8 0.6 pad.24
  1.3 0.0 copy-done.3
  1.4 0.0 copy-start.7
  1.4 0.0 copy-start.2
  1.4 0.6 copy-done.4
  2.1 0.0 copy-done.5
  2.1 0.0 copy-done.6
  2.1 0.0 copy-done.7
  2.1 0.0 copy-done.2
  2.1 0.1 reshape.90
  2.3 0.0 copy-start.1
  2.3 0.7 reshape.91.b_in
  2.9 0.1 stack.81
  3.0 0.1 fusion.15
  3.1 0.1 copy-done.1
  3.2 0.1 fusion.16
  3.3 0.1 pad_convert_fusion.2
  3.3 0.1 pad_bitcast_fusion.2
  3.5 0.1 copy.26
  3.7 0.7 copy.34
  4.3 0.1 pad_convert_fusion
  4.4 0.1 pad_bitcast_fusion
  4.6 0.1 copy.27
  4.7 0.0 copy-start.8
  4.7 0.7 copy.35
  5.4 0.0 copy-done.8
  5.4 0.7 reshape_reshape.4.bias2
  6.1 1.2 %copy.28.vecs = f32[1536,5]{1,0:T(8,128)} copy(f32[1536,5]{0,1:T(8,128)S(1)} %stack.81) | data formatting | bytes 61440 | tf_op jit(solution)/shard_map/stack | solution.py:567
  7.3 87.5 %block.1 = bf16[1536,256]{1,0:T(8,128)(2,1)} custom-call(bf16[1536,256]{1,0:T(8,128)(2,1)} %bitcast.59, f32[1536,5]{1,0:T(8,128)} %copy.28.vecs, f32[1,1536]{1,0:T(1,128)} %reshape.91.b_in, bf16[192,1536]{1,0:T(8,128)(2,1)} %bitcast.60, bf16[192,1536]{1,0:T(8,128)(2,1)} %wout.1, bf16[256,256]{1,0:T(8,128)(2,1)} %bitcast.61, bf16[192,256]{1,0:T(8,128)(2,1)} %bitcast.64, ...), custom_call_target="tpu_custom_call" | custom-call | tf_op jit(solution)/shard_map/block/pallas_call | solution.py:571
  94.8 2.1 %copy.37 = bf16[1,1536,256]{2,1,0:T(8,128)(2,1)} copy(bf16[1,1536,256]{2,1,0:T(8,128)(2,1)} %bitcast.58) | data formatting | bytes 1572864
  (25 shorter events, 0.2 us)
Async XLA Ops:
  0.0 0.7 copy-start.9
  0.0 1.3 %copy-start.3 = (f32[1536]{0:T(1024)S(1)}, f32[1536]{0:T(1024)}, u32[]{:S(2)}) copy-start(f32[1536]{0:T(1024)} %param.16) | copy-start | bytes 18436
  1.3 0.7 copy-start.4
  1.4 0.7 copy-start.5
  1.4 0.7 copy-start.6
  1.4 0.7 copy-start.7
  1.4 0.8 copy-start.2
  2.0 1.0 copy-start
  2.3 0.9 copy-start.1
  4.7 0.7 copy-start.8

commit v3 on v2

--- a/solution.py
+++ b/solution.py
@@ -35,7 +35,7 @@
     inverse = np.zeros((512, TOK))
     inverse[:MODES] = (cos * weight).T
     inverse[256 : 256 + MODES] = -(sin * weight).T
-    return jnp.asarray(forward, BF16), jnp.asarray(inverse, BF16)
+    return jnp.asarray(forward, F32), jnp.asarray(inverse, F32)
 
 
 def turned(value, step, sign):
@@ -69,25 +69,17 @@
     return out
 
 
-def erf(v):
-    x = jnp.clip(v, -3.832506856900711, 3.832506856900711)
-    s = x * x
-    p = -2.72614225801306e-10 * s + 2.77068142495902e-08
-    p = p * s - 2.10102402082508e-06
-    p = p * s - 5.69250639462346e-05
-    p = p * s - 7.34990630326855e-04
-    p = p * s - 2.95459980854025e-03
-    p = p * s - 1.60960333262415e-02
-    q = -1.45660718464996e-05 * s - 2.13374055278905e-04
-    q = q * s - 1.68282697438203e-03
-    q = q * s - 7.37332916720468e-03
-    q = q * s - 1.42647390514189e-02
-    return x * p / q
-
-
 def gelu(v):
-    half = 0.5 * v
-    return half + half * erf(v * 0.7071067811865476)
+    size = jnp.abs(v)
+    d = 1.0 + (0.3275911 * 0.7071067811865476) * size
+    t = pl.reciprocal(d, approx=True)
+    t = t * (2.0 - d * t)
+    e = jnp.exp2(v * v * (-0.5 * 1.4426950408889634))
+    q = 0.5 * 1.061405429 * t - 0.5 * 1.453152027
+    q = q * t + 0.5 * 1.421413741
+    q = q * t - 0.5 * 0.284496736
+    q = q * t + 0.5 * 0.254829592
+    return jnp.maximum(v, 0.0) - (q * t) * (e * size)
 
 
 def shrink(v):
@@ -102,18 +94,18 @@
     return jnp.dot(a, b, preferred_element_type=F32)
 
 
-def loop(n, body):
+def loop(n, body, unroll=1, start=0):
     def step(i, carry):
         body(i)
         return carry
 
-    lax.fori_loop(0, n, step, 0)
+    lax.fori_loop(start, n, step, 0, unroll=unroll)
 
 
 def kernel(
-    fields, vecs, b_in, win, wout, mix1, mix2, bias1, bias2, fwd, inv, out,
+    fields, gain1, shift1, gain2, shift2, b_out, b_in, win, wout, w1, b1, w2, b2, fwd_table, inv_table, out,
     normed, recv1, plane, mid, back, fil, recv2, hid, zt, act, part, precv, own_t,
-    w_all,
+    w_all, tile, row, mix1, mix2, bias1, bias2, units_bias, fwd, inv,
     s1, r1, s2, r2, loc, zs, zr, ps, pr,
     zws, zwr, xs, xr, ys, yr, y2s, y2r, ays, ayr, axs, axr, ax2s, ax2r,
 ):
@@ -178,40 +170,84 @@
     for copy in keeps:
         copy.start()
 
+    tile[...] = jnp.zeros_like(tile)
+    row[...] = jnp.zeros_like(row)
+
+    def diagonal(w, ri):
+        tile[0, pl.ds(0, HALF), pl.ds(0, HALF)] = w[ri, 0]
+        tile[1, pl.ds(HALF, HALF), pl.ds(0, HALF)] = w[ri, 1]
+        return tile[0] + pltpu.roll(tile[1], HALF, 1)
+
+    def bias_row(b, ri):
+        row[pl.ds(0, 1), pl.ds(0, HALF)] = b[ri, pl.ds(0, 1)]
+        row[pl.ds(8, 1), pl.ds(0, HALF)] = b[ri, pl.ds(1, 1)]
+        both = row[pl.ds(0, 8), :] + pltpu.roll(row[pl.ds(8, 8), :], HALF, 1)
+        return both[0:1]
+
+    low, high = pl.ds(0, 128), pl.ds(128, 128)
+    re, im = diagonal(w1, 0), diagonal(w1, 1)
+    mix1[low, low], mix1[low, high] = re.astype(BF16), im.astype(BF16)
+    mix1[high, low], mix1[high, high] = (-im).astype(BF16), re.astype(BF16)
+    re, im = diagonal(w2, 0).T[:CH], diagonal(w2, 1).T[:CH]
+    mix2[pl.ds(0, CH), low], mix2[pl.ds(0, CH), high] = re.astype(BF16), (-im).astype(BF16)
+    mix2[pl.ds(CH, CH), low], mix2[pl.ds(CH, CH), high] = im.astype(BF16), re.astype(BF16)
+    for ri in range(2):
+        bias1[:, pl.ds(128 * ri, 128)] = bias_row(b1, ri)
+        down = jnp.broadcast_to(bias_row(b2, ri), (128, 128)).T[:CH]
+        bias2[pl.ds(CH * ri, CH), low] = down
+        bias2[pl.ds(CH * ri, CH), pl.ds(128, 16)] = down[:, :16]
+
+    fwd[...] = fwd_table[...].astype(BF16)
+    inv[...] = inv_table[...].astype(BF16)
+    lane = lax.broadcasted_iota(jnp.int32, (1, 768), 1)
+    for g in range(4):
+        six = jnp.concatenate([b_in[pl.ds(6 * g + i, 1), :] for i in range(6)], axis=1)
+        six = jnp.where(core == 0, six, pltpu.roll(six, 768 - CH, 1))
+        half = six
+        for k in (1, 2, 3):
+            half = jnp.where(lane < CH * k, half, pltpu.roll(six, 768 - CH * k, 1))
+        units_bias[g, pl.ds(0, 1), :] = half[:, :384]
+
     def rows(i):
         return pl.ds(pl.multiple_of(i * CH, CH), CH)
 
-    def norm(load, gain_at, write):
+    def chunk(i):
+        return pl.ds(pl.multiple_of(i * 128, 128), 128)
+
+    def column(vec, i):
+        return jnp.broadcast_to(vec[pl.ds(i, 1), :], (128, 128)).T
+
+    def norm(load, gains, shifts, write):
         def add(i, acc):
-            return acc + jnp.sum(load(i).reshape(CH // 8, 8, TOK), axis=0)
-
-        total = lax.fori_loop(0, 16, add, jnp.zeros((8, TOK), F32))
+            return acc + jnp.sum(load(i).reshape(16, 8, TOK), axis=0)
+
+        total = lax.fori_loop(0, 12, add, jnp.zeros((8, TOK), F32))
         mean = jnp.sum(total, axis=0, keepdims=True) * (1.0 / D)
 
         def add_square(i, acc):
             c = load(i) - mean
-            return acc + jnp.sum((c * c).reshape(CH // 8, 8, TOK), axis=0)
-
-        total = lax.fori_loop(0, 16, add_square, jnp.zeros((8, TOK), F32))
+            return acc + jnp.sum((c * c).reshape(16, 8, TOK), axis=0)
+
+        total = lax.fori_loop(0, 12, add_square, jnp.zeros((8, TOK), F32))
         var = jnp.sum(total, axis=0, keepdims=True) * (1.0 / D)
         scale = lax.rsqrt(var + 1e-05)
 
         def finish(i):
-            v = vecs[rows(i), :]
-            c = load(i) - mean
-            gain, shift = v[:, gain_at : gain_at + 1], v[:, gain_at + 1 : gain_at + 2]
-            write(i, (c * scale * gain + shift).astype(BF16))
-
-        loop(16, finish)
+            c = (load(i) - mean) * scale
+            gain, shift = column(gains, i), column(shifts, i)
+            for at in (slice(0, 128), slice(128, 256)):
+                write(i, at, (c[:, at] * gain + shift).astype(BF16))
+
+        loop(12, finish)
 
     def load_fields(i):
-        return fields[rows(i), :].astype(F32)
-
-    def write_normed(i, v):
-        normed[rows(i), :] = v
+        return fields[chunk(i), :].astype(F32)
+
+    def write_normed(i, at, v):
+        normed[chunk(i), at] = v
 
     with jax.named_scope("norm1"):
-        norm(load_fields, 0, write_normed)
+        norm(load_fields, gain1, shift1, write_normed)
     with jax.named_scope("greet_wait"):
         pl.semaphore_wait(barrier, 22)
 
@@ -261,8 +297,12 @@
 
     for copy in keeps:
         copy.wait()
-    for k in (1, 2, 3):
-        z_move(k, False).start()
+    def start_z():
+        for k in (1, 2, 3):
+            z_move(k, False).start()
+
+    with jax.named_scope("start_z"):
+        start_z()
     with jax.named_scope("blocks_send"):
         loop(15, lambda i: to_block(15 - i).start())
     keep = pltpu.make_async_copy(normed.at[rows(chan)], recv1.at[chan, pl.ds(0, CH)], loc.at[0, 3])
@@ -272,7 +312,8 @@
         y_move(k, 0, False).start()
         y_move(k, 1, False).start()
 
-    start_y(0)
+    with jax.named_scope("start_y"):
+        start_y(0)
 
     def service_z():
         for k in (1, 2, 3):
@@ -333,15 +374,19 @@
         service_x()
     with jax.named_scope("service_a"):
         service_a()
-    with jax.named_scope("blocks_wait"):
-        loop(15, lambda i: from_plane(15 - i).wait_recv())
-
     def planes(p):
         both = recv1[pl.ds(2 * p, 2)].reshape(256, TOK)
         plane[p] = dot_nt(fwd[...], both)
 
+    def planes_in(i):
+        from_plane(2 * i).wait_recv()
+        from_plane(2 * i + 1).wait_recv()
+        planes(peer(2 * i, -1) // 2)
+
     with jax.named_scope("planes"):
-        loop(8, planes)
+        from_plane(1).wait_recv()
+        planes(chan // 2)
+        loop(8, planes_in, start=1)
 
 
     def lines(t):
@@ -357,7 +402,7 @@
             plane[a // 2, im_at, lanes] = im
 
     with jax.named_scope("lines"):
-        loop(18, lines)
+        loop(18, lines, unroll=2)
 
     def mix(p):
         v = plane[p].astype(BF16)
@@ -386,7 +431,7 @@
             back[a, im_at, lanes] = im
 
     with jax.named_scope("lines_back"):
-        loop(24, lines_back)
+        loop(24, lines_back, unroll=2)
 
     def planes_back(p):
         lhs = [
@@ -398,16 +443,21 @@
             v = res[i * CH : (i + 1) * CH] + recv1[2 * p + i, pl.ds(0, CH), :].astype(F32)
             fil[2 * p + i] = v.astype(BF16)
 
-    with jax.named_scope("planes_back"):
-        loop(8, planes_back)
-
     def to_plane(j):
         return remote(fil.at[peer(j, 1)], recv2.at[rows(chan)], s2.at[j], r2.at[j], (peer(j, 1), batch))
 
     def from_block(j):
         return remote(fil.at[chan], recv2.at[rows(peer(j, -1))], s2.at[j], r2.at[j], (peer(j, 1), batch))
 
-    loop(15, lambda i: to_plane(15 - i).start())
+    def planes_out(i):
+        planes_back(peer(14 - 2 * i, 1) // 2)
+        to_plane(14 - 2 * i).start()
+        to_plane(15 - 2 * i).start()
+
+    with jax.named_scope("planes_back"):
+        loop(7, planes_out)
+        planes_back(chan // 2)
+    to_plane(1).start()
     keep = pltpu.make_async_copy(fil.at[chan], recv2.at[rows(chan)], loc.at[1, 3])
     keep.start()
     with jax.named_scope("service_y1"):
@@ -421,19 +471,19 @@
         loop(15, lambda i: from_block(15 - i).wait_recv())
 
     def hidden(i):
-        hid[rows(i), :] = load_fields(i) + recv2[rows(i), :].astype(F32)
+        hid[chunk(i), :] = load_fields(i) + recv2[chunk(i), :].astype(F32)
 
     with jax.named_scope("hidden"):
-        loop(16, hidden)
-
-    def write_z(i, v):
-        recv2[rows(i), :] = v
+        loop(12, hidden)
+
+    def write_z(i, at, v):
+        recv2[chunk(i), at] = v
 
     def load_hidden(i):
-        return hid[rows(i), :]
+        return hid[chunk(i), :]
 
     with jax.named_scope("norm2"):
-        norm(load_hidden, 2, write_z)
+        norm(load_hidden, gain2, shift2, write_z)
 
     eye = (
         lax.broadcasted_iota(jnp.int32, (TOK, TOK), 0) == lax.broadcasted_iota(jnp.int32, (TOK, TOK), 1)
@@ -460,7 +510,7 @@
         res = dot_nt(zt[t], w)
         for n in range(2):
             at = pl.ds(pl.multiple_of(g[n] * 384, 128), 384)
-            act[t, :, at] = gelu(res[:, n * 384 : (n + 1) * 384] + b_in[:, at]).astype(BF16)
+            act[t, :, at] = gelu(res[:, n * 384 : (n + 1) * 384] + units_bias[g[n], pl.ds(0, 1), :]).astype(BF16)
 
     with jax.named_scope("win_wait_a"):
         for k in (2, 3):
@@ -518,7 +568,9 @@
     def finish(i):
         at = pl.ds(pl.multiple_of(i * 128, 128), 128)
         total = (own_t[:, at] + precv[:, at].astype(F32)).T
-        out[at, :] = (hid[at, :] + total + vecs[at, :][:, 4:5]).astype(BF16)
+        shift = column(b_out, i)
+        for to in (slice(0, 128), slice(128, 256)):
+            out[at, to] = (hid[at, to] + total[:, to] + shift).astype(BF16)
 
     with jax.named_scope("finish"):
         loop(12, finish)
@@ -527,51 +579,37 @@
     loop(15, lambda i: to_plane(15 - i).wait_send())
     send_z.wait_send()
     send_part.wait_send()
-    for k in range(4):
-        if k:
-            z_move(k, False).wait_send()
-            ay(k, False).wait_send()
-            for way in range(3):
-                x_move(k, way, False).wait_send()
-        for way in range(2):
-            y_move(k, way, False).wait_send()
-            ax(k, way, False).wait_send()
-        y_pass(k, False).wait_send()
-        ax_pass(k, False).wait_send()
-
-
-def blocks_matrix(w, b):
-    def diag(m):
-        zero = jnp.zeros((HALF, HALF), F32)
-        top = jnp.concatenate([m[0], zero], axis=1)
-        low = jnp.concatenate([zero, m[1]], axis=1)
-        return jnp.concatenate([top, low], axis=0)
-
-    re, im = diag(w[0]), diag(w[1])
-    full = jnp.stack([jnp.stack([re, im]), jnp.stack([-im, re])])
-    return full, b.reshape(2, CH)
+    def sent():
+        for k in range(4):
+            if k:
+                z_move(k, False).wait_send()
+                ay(k, False).wait_send()
+                for way in range(3):
+                    x_move(k, way, False).wait_send()
+            for way in range(2):
+                y_move(k, way, False).wait_send()
+                ax(k, way, False).wait_send()
+            y_pass(k, False).wait_send()
+            ax_pass(k, False).wait_send()
+
+    with jax.named_scope("sent"):
+        sent()
 
 
 def on_device(
     fields, norm1_gain, norm1_shift, spec_w1, spec_b1, spec_w2, spec_b2,
     norm2_gain, norm2_shift, w_in, b_in, w_out, b_out,
 ):
-    core = lax.axis_index("chan") % 2
     forward, inverse = plane_tables()
-    m1, c1 = blocks_matrix(spec_w1, spec_b1)
-    m1 = jnp.pad(m1, ((0, 0), (0, 0), (0, 32), (0, 32))).transpose(0, 2, 1, 3).reshape(256, 256)
-    c1 = jnp.pad(c1, ((0, 0), (0, 32))).reshape(1, 256)
-    m2, c2 = blocks_matrix(spec_w2, spec_b2)
-    m2 = jnp.pad(m2, ((0, 0), (0, 0), (0, 32), (0, 0))).transpose(1, 3, 0, 2).reshape(192, 256)
-    c2 = c2.reshape(192, 1)
-    vecs = jnp.stack([norm1_gain, norm1_shift, norm2_gain, norm2_shift, b_out], axis=1)
-    units_bias = lax.dynamic_slice(b_in.reshape(16, 2, CH), (0, core, 0), (16, 1, CH)).reshape(1, D)
+    gain1, shift1, gain2, shift2, last = (
+        v.reshape(12, 128) for v in (norm1_gain, norm1_shift, norm2_gain, norm2_shift, b_out)
+    )
     vmem = pl.BlockSpec(memory_space=pltpu.VMEM)
     dma = pltpu.SemaphoreType.DMA
     res = pl.pallas_call(
         kernel,
         out_shape=jax.ShapeDtypeStruct((D, TOK), BF16),
-        in_specs=[vmem] * 3 + [pl.BlockSpec(memory_space=pl.ANY)] * 2 + [vmem] * 6,
+        in_specs=[vmem] * 7 + [pl.BlockSpec(memory_space=pl.ANY)] * 2 + [vmem] * 6,
         out_specs=vmem,
         scratch_shapes=[
             pltpu.VMEM((D, TOK), BF16),
@@ -588,6 +626,15 @@
             pltpu.VMEM((TOK, D), BF16),
             pltpu.VMEM((TOK, D), F32),
             pltpu.VMEM((4, 16, CH, 768), BF16),
+            pltpu.VMEM((2, 128, 128), F32),
+            pltpu.VMEM((16, 128), F32),
+            pltpu.VMEM((256, 256), BF16),
+            pltpu.VMEM((2 * CH, 256), BF16),
+            pltpu.VMEM((1, 256), F32),
+            pltpu.VMEM((2 * CH, MODES), F32),
+            pltpu.VMEM((4, 8, 384), F32),
+            pltpu.VMEM((2 * MODES, TOK), BF16),
+            pltpu.VMEM((512, TOK), BF16),
             dma((16,)), dma((16,)), dma((16,)), dma((16,)), dma((4, 4)),
             dma, dma, dma, dma,
             dma((4,)), dma((4,)), dma((3, 4)), dma((3, 4)), dma((2, 4)), dma((2, 4)), dma((4,)), dma((4,)),
@@ -598,7 +645,8 @@
         ),
         name="block",
     )(
-        fields[0], vecs, units_bias, w_in.T, w_out, m1.astype(BF16), m2.astype(BF16), c1, c2, forward, inverse
+        fields[0], gain1, shift1, gain2, shift2, last, b_in.reshape(24, 128), w_in.T, w_out,
+        spec_w1, spec_b1, spec_w2, spec_b2, forward, inverse,
     )
     return res[None]
 

time: 98.3 us -> 90.6 us (0.922)
  local copies, waits for them, and re-layouts: 8.89 us -> 2.06 us
    unnamed x23 -> x1, local copies, waits for them, and re-layouts: 4.83 us -> 2.06 us
    another operation x10 -> x0, local copies, waits for them, and re-layouts: 2.18 us -> none  [the longest x7 1.27 us: on_device(): jnp.stack([norm1_gain, norm1_shift, norm2_gain, norm2_shift, b_out], axis=1)]
where the time goes in v3:
time: 90.6 us; the launch traced here: 89.2 us
  Pallas kernels  87.1 us (96%)
  local copies, waits for them, and re-layouts  2.06 us (2%)
    pallas_call x1, Pallas kernels, on_device(): pl.pallas_call(kernel, out_shape=jax.ShapeDtypeStruct((D, TOK), BF16), in...  87.1 us
    unnamed x1, local copies, waits for them, and re-layouts  2.06 us

profile of v3, /device:TPU:1, one launch (start us, length us, event | category | flops | bytes accessed | tf_op | source)
XLA Modules:
  0.0 89.2 jit_solution(16282493478302081306)
XLA Ops:
  0.0 87.1 %block.1 = bf16[1536,256]{1,0:T(8,128)(2,1)} custom-call(bf16[1536,256]{1,0:T(8,128)(2,1)} %bitcast.10, f32[12,128]{1,0:T(8,128)} %bitcast.13, f32[12,128]{1,0:T(8,128)} %bitcast.14, f32[12,128]{1,0:T(8,128)} %bitcast.15, f32[12,128]{1,0:T(8,128)} %bitcast.16, f32[12,128]{1,0:T(8,128)} %bitcast.17, f32[24,128]{1,0:T(8,128)} %bitcast.12, ...), custom_call_target="tpu_custom_call" | custom-call | tf_op jit(solution)/shard_map/block/pallas_call | solution.py:609
  87.1 2.1 %copy.17 = bf16[1,1536,256]{2,1,0:T(8,128)(2,1)} copy(bf16[1,1536,256]{2,1,0:T(8,128)(2,1)} %bitcast.9) | data formatting | bytes 1572864

commit v4 on v3

--- a/solution.py
+++ b/solution.py
@@ -105,7 +105,7 @@
 def kernel(
     fields, gain1, shift1, gain2, shift2, b_out, b_in, win, wout, w1, b1, w2, b2, fwd_table, inv_table, out,
     normed, recv1, plane, mid, back, fil, recv2, hid, zt, act, part, precv, own_t,
-    w_all, tile, row, mix1, mix2, bias1, bias2, units_bias, fwd, inv,
+    w_wide, w_slim, tile, row, mix1, mix2, bias1, bias2, units_bias, fwd, inv,
     s1, r1, s2, r2, loc, zs, zr, ps, pr,
     zws, zwr, xs, xr, ys, yr, y2s, y2r, ays, ayr, axs, axr, ax2s, ax2r,
 ):
@@ -153,23 +153,164 @@
     own_slot = slot(0, 0)
     mine = pl.ds(pl.multiple_of(core * CH, CH), CH)
     keeps = []
-    for q in range(4):
-        for n, (src, at, size, to) in enumerate(
-            ((win, 384 * q, 384, 0), (wout, 1024 + 128 * q, 128, 384))
-        ):
+    for ph, src in enumerate((win, wout)):
+        for q in range(4):
             keeps.append(
-                pltpu.make_async_copy(
-                    src.at[mine, pl.ds(at, size)], w_all.at[q, own_slot, :, pl.ds(to, size)], loc.at[q, n]
-                )
+                pltpu.make_async_copy(src.at[mine, pl.ds(384 * q, 256)], w_wide.at[ph, q, own_slot], loc.at[ph, q])
             )
-    keeps.append(
-        pltpu.make_async_copy(
-            wout.at[mine, pl.ds(pl.multiple_of(256 * x, 128), 256)], w_all.at[x, own_slot, :, pl.ds(512, 256)], loc.at[2, 3]
-        )
-    )
+        at = pl.ds(pl.multiple_of(384 * x + 256, 128), 128)
+        keeps.append(pltpu.make_async_copy(src.at[mine, at], w_slim.at[ph, x, own_slot], loc.at[ph, 4]))
     for copy in keeps:
         copy.start()
 
+    def rows(i):
+        return pl.ds(pl.multiple_of(i * CH, CH), CH)
+
+    def chunk(i):
+        return pl.ds(pl.multiple_of(i * 128, 128), 128)
+
+    def column(vec, i):
+        return jnp.broadcast_to(vec[pl.ds(i, 1), :], (128, 128)).T
+
+    def norm(load, gains, shifts, write, total=None):
+        def add(i, acc):
+            return acc + jnp.sum(load(i).reshape(16, 8, TOK), axis=0)
+
+        if total is None:
+            total = lax.fori_loop(0, 12, add, jnp.zeros((8, TOK), F32))
+        mean = jnp.sum(total, axis=0, keepdims=True) * (1.0 / D)
+
+        def add_square(i, acc):
+            c = load(i) - mean
+            return acc + jnp.sum((c * c).reshape(16, 8, TOK), axis=0)
+
+        total = lax.fori_loop(0, 12, add_square, jnp.zeros((8, TOK), F32))
+        var = jnp.sum(total, axis=0, keepdims=True) * (1.0 / D)
+        scale = lax.rsqrt(var + 1e-05)
+
+        def finish(i):
+            c = (load(i) - mean) * scale
+            gain, shift = column(gains, i), column(shifts, i)
+            for at in (slice(0, 128), slice(128, 256)):
+                write(i, at, (c[:, at] * gain + shift).astype(BF16))
+
+        loop(12, finish)
+
+    def load_fields(i):
+        return fields[chunk(i), :].astype(F32)
+
+    def write_normed(i, at, v):
+        normed[chunk(i), at] = v
+
+    with jax.named_scope("norm1"):
+        norm(load_fields, gain1, shift1, write_normed)
+    with jax.named_scope("greet_wait"):
+        pl.semaphore_wait(barrier, 22)
+
+    def to_block(j):
+        return remote(
+            normed.at[rows(peer(j, 1))], recv1.at[chan, pl.ds(0, CH)], s1.at[j], r1.at[j], (peer(j, 1), batch)
+        )
+
+    def from_plane(j):
+        return remote(
+            normed.at[rows(chan)], recv1.at[peer(j, -1), pl.ds(0, CH)], s1.at[j], r1.at[j], (peer(j, 1), batch)
+        )
+
+    def z_move(ph, k, wide, came):
+        ref = w_wide if wide else w_slim
+        at = ref.at[ph, x, slot(0, k if came else 0)]
+        to = {1: zp, 2: zm, 3: dev(x, y, z + 2 + 4 * core, core)}[k]
+        return remote(at, at, zws.at[ph, wide, k], zwr.at[ph, wide, k], to)
+
+    def x_move(ph, k, way, came):
+        at = w_wide.at[ph, (x + ((3, 1, 2)[way] if came else 0)) % 4, slot(0, k)]
+        return remote(at, at, xs.at[ph, way, k], xr.at[ph, way, k], (xp, xm, x2)[way])
+
+    def y_move(ph, k, way, came):
+        at = w_wide.at[ph, :, slot((3, 1)[way] if came else 0, k)]
+        return remote(at, at, ys.at[ph, way, k], yr.at[ph, way, k], (yp, ym)[way])
+
+    def y_pass(ph, k, came):
+        at = w_wide.at[ph, :, slot(2 if came else (3 if k < 2 else 1), k)]
+        return remote(at, at, y2s.at[ph, k], y2r.at[ph, k], yp if k < 2 else ym)
+
+    def group(ph, q, dy):
+        return w_slim.at[ph, q, pl.ds(((y + dy) % 4) * 4, 4)]
+
+    def ay(ph, r, came):
+        at = group(ph, x, offs[r] if came else 0)
+        return remote(at, at, ays.at[ph, r], ayr.at[ph, r], {1: yp, 2: ym, 3: y2}[r])
+
+    def ax(ph, r, way, came):
+        at = group(ph, (x + ((3, 1)[way] if came else 0)) % 4, offs[r])
+        return remote(at, at, axs.at[ph, way, r], axr.at[ph, way, r], (xp, xm)[way])
+
+    def ax_pass(ph, r, came):
+        at = group(ph, (x + (2 if came else (3 if r < 2 else 1))) % 4, offs[r])
+        return remote(at, at, ax2s.at[ph, r], ax2r.at[ph, r], xp if r < 2 else xm)
+
+    def start_z(ph):
+        for k in (1, 2, 3):
+            z_move(ph, k, 1, False).start()
+            z_move(ph, k, 0, False).start()
+
+    def start_y(ph, k):
+        y_move(ph, k, 0, False).start()
+        y_move(ph, k, 1, False).start()
+
+    for copy in keeps:
+        copy.wait()
+    with jax.named_scope("start_z"):
+        start_z(0)
+        start_z(1)
+    with jax.named_scope("blocks_send"):
+        loop(8, lambda i: to_block(15 - i).start())
+    keep = pltpu.make_async_copy(normed.at[rows(chan)], recv1.at[chan, pl.ds(0, CH)], loc.at[0, 5])
+    keep.start()
+
+    with jax.named_scope("start_y"):
+        start_y(0, 0)
+        start_y(1, 0)
+    loop(7, lambda i: to_block(7 - i).start())
+
+    def service_z(ph):
+        for k in (1, 2, 3):
+            z_move(ph, k, 1, True).wait_recv()
+            for way in range(3):
+                x_move(ph, k, way, False).start()
+            z_move(ph, k, 0, True).wait_recv()
+        for r in (1, 2, 3):
+            ay(ph, r, False).start()
+        ax(ph, 0, 0, False).start()
+        ax(ph, 0, 1, False).start()
+
+    def service_x(ph):
+        for k in (1, 2, 3):
+            for way in range(3):
+                x_move(ph, k, way, True).wait_recv()
+            start_y(ph, k)
+
+    def service_a(ph):
+        for r in (1, 2, 3):
+            ay(ph, r, True).wait_recv()
+            ax(ph, r, 0, False).start()
+            ax(ph, r, 1, False).start()
+
+    def service_y(ph, ks):
+        for k in ks:
+            y_move(ph, k, 0 if k < 2 else 1, True).wait_recv()
+            y_pass(ph, k, False).start()
+
+    def service_ax(ph):
+        for r in range(4):
+            ax(ph, r, 0 if r < 2 else 1, True).wait_recv()
+            ax_pass(ph, r, False).start()
+
+    with jax.named_scope("service_1"):
+        service_z(0)
+        service_y(0, (0,))
+        service_z(1)
     tile[...] = jnp.zeros_like(tile)
     row[...] = jnp.zeros_like(row)
 
@@ -208,160 +349,6 @@
             half = jnp.where(lane < CH * k, half, pltpu.roll(six, 768 - CH * k, 1))
         units_bias[g, pl.ds(0, 1), :] = half[:, :384]
 
-    def rows(i):
-        return pl.ds(pl.multiple_of(i * CH, CH), CH)
-
-    def chunk(i):
-        return pl.ds(pl.multiple_of(i * 128, 128), 128)
-
-    def column(vec, i):
-        return jnp.broadcast_to(vec[pl.ds(i, 1), :], (128, 128)).T
-
-    def norm(load, gains, shifts, write):
-        def add(i, acc):
-            return acc + jnp.sum(load(i).reshape(16, 8, TOK), axis=0)
-
-        total = lax.fori_loop(0, 12, add, jnp.zeros((8, TOK), F32))
-        mean = jnp.sum(total, axis=0, keepdims=True) * (1.0 / D)
-
-        def add_square(i, acc):
-            c = load(i) - mean
-            return acc + jnp.sum((c * c).reshape(16, 8, TOK), axis=0)
-
-        total = lax.fori_loop(0, 12, add_square, jnp.zeros((8, TOK), F32))
-        var = jnp.sum(total, axis=0, keepdims=True) * (1.0 / D)
-        scale = lax.rsqrt(var + 1e-05)
-
-        def finish(i):
-            c = (load(i) - mean) * scale
-            gain, shift = column(gains, i), column(shifts, i)
-            for at in (slice(0, 128), slice(128, 256)):
-                write(i, at, (c[:, at] * gain + shift).astype(BF16))
-
-        loop(12, finish)
-
-    def load_fields(i):
-        return fields[chunk(i), :].astype(F32)
-
-    def write_normed(i, at, v):
-        normed[chunk(i), at] = v
-
-    with jax.named_scope("norm1"):
-        norm(load_fields, gain1, shift1, write_normed)
-    with jax.named_scope("greet_wait"):
-        pl.semaphore_wait(barrier, 22)
-
-    def to_block(j):
-        return remote(
-            normed.at[rows(peer(j, 1))], recv1.at[chan, pl.ds(0, CH)], s1.at[j], r1.at[j], (peer(j, 1), batch)
-        )
-
-    def from_plane(j):
-        return remote(
-            normed.at[rows(chan)], recv1.at[peer(j, -1), pl.ds(0, CH)], s1.at[j], r1.at[j], (peer(j, 1), batch)
-        )
-
-    first, last = pl.ds(0, 512), pl.ds(512, 256)
-
-    def z_move(k, came):
-        at = w_all.at[x, slot(0, k if came else 0)]
-        to = {1: zp, 2: zm, 3: dev(x, y, z + 2 + 4 * core, core)}[k]
-        return remote(at, at, zws.at[k], zwr.at[k], to)
-
-    def x_move(k, way, came):
-        at = w_all.at[(x + ((3, 1, 2)[way] if came else 0)) % 4, slot(0, k), :, first]
-        return remote(at, at, xs.at[way, k], xr.at[way, k], (xp, xm, x2)[way])
-
-    def y_move(k, way, came):
-        at = w_all.at[:, slot((3, 1)[way] if came else 0, k), :, first]
-        return remote(at, at, ys.at[way, k], yr.at[way, k], (yp, ym)[way])
-
-    def y_pass(k, came):
-        at = w_all.at[:, slot(2 if came else (3 if k < 2 else 1), k), :, first]
-        return remote(at, at, y2s.at[k], y2r.at[k], yp if k < 2 else ym)
-
-    def group(q, dy):
-        return w_all.at[q, pl.ds(((y + dy) % 4) * 4, 4), :, last]
-
-    def ay(r, came):
-        at = group(x, offs[r] if came else 0)
-        return remote(at, at, ays.at[r], ayr.at[r], {1: yp, 2: ym, 3: y2}[r])
-
-    def ax(r, way, came):
-        at = group((x + ((3, 1)[way] if came else 0)) % 4, offs[r])
-        return remote(at, at, axs.at[way, r], axr.at[way, r], (xp, xm)[way])
-
-    def ax_pass(r, came):
-        at = group((x + (2 if came else (3 if r < 2 else 1))) % 4, offs[r])
-        return remote(at, at, ax2s.at[r], ax2r.at[r], xp if r < 2 else xm)
-
-    for copy in keeps:
-        copy.wait()
-    def start_z():
-        for k in (1, 2, 3):
-            z_move(k, False).start()
-
-    with jax.named_scope("start_z"):
-        start_z()
-    with jax.named_scope("blocks_send"):
-        loop(15, lambda i: to_block(15 - i).start())
-    keep = pltpu.make_async_copy(normed.at[rows(chan)], recv1.at[chan, pl.ds(0, CH)], loc.at[0, 3])
-    keep.start()
-
-    def start_y(k):
-        y_move(k, 0, False).start()
-        y_move(k, 1, False).start()
-
-    with jax.named_scope("start_y"):
-        start_y(0)
-
-    def service_z():
-        for k in (1, 2, 3):
-            z_move(k, True).wait_recv()
-            for way in range(3):
-                x_move(k, way, False).start()
-        for r in (1, 2, 3):
-            ay(r, False).start()
-        ax(0, 0, False).start()
-        ax(0, 1, False).start()
-
-    def service_y0():
-        y_move(0, 0, True).wait_recv()
-        y_pass(0, False).start()
-
-    def service_x():
-        for k in (1, 2, 3):
-            for way in range(3):
-                x_move(k, way, True).wait_recv()
-            start_y(k)
-
-    def service_a():
-        for r in (1, 2, 3):
-            ay(r, True).wait_recv()
-            ax(r, 0, False).start()
-            ax(r, 1, False).start()
-
-    def service_y1():
-        y_move(1, 0, True).wait_recv()
-        y_pass(1, False).start()
-
-    def service_y2():
-        for k in (2, 3):
-            y_move(k, 1, True).wait_recv()
-            y_pass(k, False).start()
-
-    def service_ax():
-        for r in (0, 1):
-            ax(r, 0, True).wait_recv()
-            ax_pass(r, False).start()
-        for r in (2, 3):
-            ax(r, 1, True).wait_recv()
-            ax_pass(r, False).start()
-
-    with jax.named_scope("service_z"):
-        service_z()
-    with jax.named_scope("service_y0"):
-        service_y0()
     def clear(a):
         recv1[a, pl.ds(CH, 32), :] = jnp.zeros((32, TOK), BF16)
         back[a, :, pl.ds(128, 128)] = jnp.zeros((2 * CH, 128), F32)
@@ -370,10 +357,15 @@
         loop(16, clear)
 
     keep.wait()
-    with jax.named_scope("service_x"):
-        service_x()
-    with jax.named_scope("service_a"):
-        service_a()
+    with jax.named_scope("service_2"):
+        service_x(0)
+        service_a(0)
+        service_y(1, (0,))
+
+    with jax.named_scope("service_3"):
+        service_x(1)
+        service_y(0, (1,))
+
     def planes(p):
         both = recv1[pl.ds(2 * p, 2)].reshape(256, TOK)
         plane[p] = dot_nt(fwd[...], both)
@@ -404,7 +396,7 @@
     with jax.named_scope("lines"):
         loop(18, lines, unroll=2)
 
-    def mix(p):
+    def mix_in(p):
         v = plane[p].astype(BF16)
         lhs = jnp.concatenate(
             [
@@ -413,13 +405,19 @@
             ],
             axis=0,
         )
-        mid[...] = gelu(dot(lhs, mix1[...]) + bias1[...]).astype(BF16)
+        mid[p] = gelu(dot(lhs, mix1[...]) + bias1[...]).astype(BF16)
+
+    def mix_out(p):
         for half in range(2):
-            res = dot_nt(mix2[...], mid[pl.ds(half * MODES, MODES), :]) + bias2[...]
+            res = dot_nt(mix2[...], mid[p, pl.ds(half * MODES, MODES), :]) + bias2[...]
             back[2 * p + half, :, pl.ds(0, MODES)] = shrink(res)
 
     with jax.named_scope("mix"):
-        loop(8, mix)
+        loop(8, mix_in, unroll=2)
+        loop(8, mix_out, unroll=2)
+    with jax.named_scope("service_4"):
+        service_y(0, (2, 3))
+        service_a(1)
 
     def lines_back(t):
         re_at = pl.ds(pl.multiple_of((t // 2) * 8, 8), 8)
@@ -458,23 +456,26 @@
         loop(7, planes_out)
         planes_back(chan // 2)
     to_plane(1).start()
-    keep = pltpu.make_async_copy(fil.at[chan], recv2.at[rows(chan)], loc.at[1, 3])
+    keep = pltpu.make_async_copy(fil.at[chan], recv2.at[rows(chan)], loc.at[1, 5])
     keep.start()
-    with jax.named_scope("service_y1"):
-        service_y1()
-    with jax.named_scope("service_ax"):
-        service_ax()
-    with jax.named_scope("service_y2"):
-        service_y2()
+    with jax.named_scope("service_5"):
+        service_y(1, (1,))
+        service_ax(0)
+        service_y(1, (2, 3))
+        service_ax(1)
     keep.wait()
+
+    def take(p, acc):
+        v = fields[rows(p), :].astype(F32) + recv2[rows(p), :].astype(F32)
+        hid[rows(p), :] = v
+        return acc + jnp.sum(v.reshape(CH // 8, 8, TOK), axis=0)
+
+    def take_next(j, acc):
+        from_block(j).wait_recv()
+        return take(peer(j, -1), acc)
+
     with jax.named_scope("filtered_wait"):
-        loop(15, lambda i: from_block(15 - i).wait_recv())
-
-    def hidden(i):
-        hid[chunk(i), :] = load_fields(i) + recv2[chunk(i), :].astype(F32)
-
-    with jax.named_scope("hidden"):
-        loop(12, hidden)
+        channel_sum = lax.fori_loop(1, 16, take_next, take(chan, jnp.zeros((8, TOK), F32)))
 
     def write_z(i, at, v):
         recv2[chunk(i), at] = v
@@ -483,7 +484,7 @@
         return hid[chunk(i), :]
 
     with jax.named_scope("norm2"):
-        norm(load_hidden, gain2, shift2, write_z)
+        norm(load_hidden, gain2, shift2, write_z, channel_sum)
 
     eye = (
         lax.broadcasted_iota(jnp.int32, (TOK, TOK), 0) == lax.broadcasted_iota(jnp.int32, (TOK, TOK), 1)
@@ -500,54 +501,64 @@
 
     def units(i, t):
         g = [(y + offs[2 * i + n]) % 4 for n in range(2)]
-        w = jnp.concatenate(
-            [
-                jnp.concatenate([w_all[q, pl.ds(g[n] * 4, 4), :, :384].reshape(384, 384) for q in range(4)], axis=1)
-                for n in range(2)
-            ],
-            axis=0,
-        )
-        res = dot_nt(zt[t], w)
+
+        def shards(n):
+            at = pl.ds(g[n] * 4, 4)
+            parts = [
+                (w_wide[0, q, at].reshape(384, 256), w_slim[0, q, at].reshape(384, 128)) for q in range(4)
+            ]
+            return jnp.concatenate([v for pair in parts for v in pair], axis=1)
+
+        res = dot_nt(zt[t], jnp.concatenate([shards(0), shards(1)], axis=0))
         for n in range(2):
             at = pl.ds(pl.multiple_of(g[n] * 384, 128), 384)
             act[t, :, at] = gelu(res[:, n * 384 : (n + 1) * 384] + units_bias[g[n], pl.ds(0, 1), :]).astype(BF16)
 
-    with jax.named_scope("win_wait_a"):
+    def arrived(ph):
+        for k in range(4):
+            y_move(ph, k, 0 if k >= 2 else 1, True).wait_recv()
+        for r in range(4):
+            ax(ph, r, 0 if r >= 2 else 1, True).wait_recv()
+        for k in range(4):
+            ax_pass(ph, k, True).wait_recv()
+        for k in range(4):
+            y_pass(ph, k, True).wait_recv()
+
+    with jax.named_scope("win_wait"):
         for k in (2, 3):
-            y_move(k, 0, True).wait_recv()
+            y_move(0, k, 0, True).wait_recv()
+        for r in range(4):
+            ax(0, r, 0 if r >= 2 else 1, True).wait_recv()
+        for k in range(4):
+            ax_pass(0, k, True).wait_recv()
     with jax.named_scope("units_own_a"):
         units(0, 0)
+    with jax.named_scope("win_wait_b"):
+        for k in (0, 1):
+            y_move(0, k, 1, True).wait_recv()
+        for k in range(4):
+            y_pass(0, k, True).wait_recv()
+    with jax.named_scope("units_own_b"):
+        units(1, 0)
     with jax.named_scope("z_wait"):
         send_z.wait_recv()
-    with jax.named_scope("units_mate_a"):
-        units(0, 1)
-    with jax.named_scope("win_wait_b"):
-        for k in (0, 1):
-            y_move(k, 1, True).wait_recv()
-        for k in range(4):
-            y_pass(k, True).wait_recv()
-    with jax.named_scope("units_mate_b"):
-        units(1, 1)
-    with jax.named_scope("units_own_b"):
-        units(1, 0)
+    with jax.named_scope("units_mate"):
+        [units(i, 1) for i in range(2)]
     with jax.named_scope("wout_wait"):
-        for r in range(4):
-            ax(r, 0 if r >= 2 else 1, True).wait_recv()
-        for r in range(4):
-            ax_pass(r, True).wait_recv()
+        arrived(1)
 
     def project(t, write):
-        def one(q):
-            write(
-                pl.ds(pl.multiple_of(q * 256, 128), 256), dot(act[t], w_all[q, :, :, 512:].reshape(D, 256))
-            )
-
-        def two(i):
-            w = jnp.concatenate([w_all[2 * i + n, :, :, 384:512].reshape(D, 128) for n in range(2)], axis=1)
-            write(pl.ds(pl.multiple_of(1024 + i * 256, 128), 256), dot(act[t], w))
-
-        loop(2, two)
-        loop(4, one)
+        def wide(q):
+            write(pl.ds(pl.multiple_of(q * 384, 128), 256), dot(act[t], w_wide[1, q].reshape(D, 256)))
+
+        def slim(i):
+            w = jnp.concatenate([w_slim[1, 2 * i + n].reshape(D, 128) for n in range(2)], axis=1)
+            res = dot(act[t], w)
+            for n in range(2):
+                write(pl.ds(pl.multiple_of((2 * i + n) * 384 + 256, 128), 128), res[:, n * 128 : (n + 1) * 128])
+
+        loop(2, slim)
+        loop(4, wide)
 
     def write_part(at, v):
         part[:, at] = v.astype(BF16)
@@ -579,21 +590,23 @@
     loop(15, lambda i: to_plane(15 - i).wait_send())
     send_z.wait_send()
     send_part.wait_send()
-    def sent():
+    def sent(ph):
         for k in range(4):
             if k:
-                z_move(k, False).wait_send()
-                ay(k, False).wait_send()
+                z_move(ph, k, 0, False).wait_send()
+                z_move(ph, k, 1, False).wait_send()
+                ay(ph, k, False).wait_send()
                 for way in range(3):
-                    x_move(k, way, False).wait_send()
+                    x_move(ph, k, way, False).wait_send()
             for way in range(2):
-                y_move(k, way, False).wait_send()
-                ax(k, way, False).wait_send()
-            y_pass(k, False).wait_send()
-            ax_pass(k, False).wait_send()
+                y_move(ph, k, way, False).wait_send()
+                ax(ph, k, way, False).wait_send()
+            y_pass(ph, k, False).wait_send()
+            ax_pass(ph, k, False).wait_send()
 
     with jax.named_scope("sent"):
-        sent()
+        sent(0)
+        sent(1)
 
 
 def on_device(
@@ -615,7 +628,7 @@
             pltpu.VMEM((D, TOK), BF16),
             pltpu.VMEM((16, 128, TOK), BF16),
             pltpu.VMEM((8, 2 * MODES, 256), F32),
-            pltpu.VMEM((2 * MODES, 256), BF16),
+            pltpu.VMEM((8, 2 * MODES, 256), BF16),
             pltpu.VMEM((16, 2 * CH, 256), F32),
             pltpu.VMEM((16, CH, TOK), BF16),
             pltpu.VMEM((D, TOK), BF16),
@@ -625,7 +638,8 @@
             pltpu.VMEM((TOK, D), BF16),
             pltpu.VMEM((TOK, D), BF16),
             pltpu.VMEM((TOK, D), F32),
-            pltpu.VMEM((4, 16, CH, 768), BF16),
+            pltpu.VMEM((2, 4, 16, CH, 256), BF16),
+            pltpu.VMEM((2, 4, 16, CH, 128), BF16),
             pltpu.VMEM((2, 128, 128), F32),
             pltpu.VMEM((16, 128), F32),
             pltpu.VMEM((256, 256), BF16),
@@ -635,10 +649,11 @@
             pltpu.VMEM((4, 8, 384), F32),
             pltpu.VMEM((2 * MODES, TOK), BF16),
             pltpu.VMEM((512, TOK), BF16),
-            dma((16,)), dma((16,)), dma((16,)), dma((16,)), dma((4, 4)),
+            dma((16,)), dma((16,)), dma((16,)), dma((16,)), dma((2, 6)),
             dma, dma, dma, dma,
-            dma((4,)), dma((4,)), dma((3, 4)), dma((3, 4)), dma((2, 4)), dma((2, 4)), dma((4,)), dma((4,)),
-            dma((4,)), dma((4,)), dma((2, 4)), dma((2, 4)), dma((4,)), dma((4,)),
+            dma((2, 2, 4)), dma((2, 2, 4)), dma((2, 3, 4)), dma((2, 3, 4)), dma((2, 2, 4)), dma((2, 2, 4)),
+            dma((2, 4)), dma((2, 4)), dma((2, 4)), dma((2, 4)), dma((2, 2, 4)), dma((2, 2, 4)),
+            dma((2, 4)), dma((2, 4)),
         ],
         compiler_params=pltpu.CompilerParams(
             collective_id=0, has_side_effects=True, vmem_limit_bytes=56 * 2**20

time: 90.6 us -> 89.3 us (0.986)
  Pallas kernels: 87.1 us -> 85.6 us
    pallas_call x1, Pallas kernels: 87.1 us -> 85.6 us  [on_device(): pl.pallas_call(kernel, out_shape=jax.ShapeDtypeStruct((D, TOK), BF16), in...]
where the time goes in v4:
time: 89.3 us; the launch traced here: 87.7 us
  Pallas kernels  85.6 us (96%)
  local copies, waits for them, and re-layouts  2.06 us (2%)
    pallas_call x1, Pallas kernels, on_device(): pl.pallas_call(kernel, out_shape=jax.ShapeDtypeStruct((D, TOK), BF16), in...  85.6 us
    unnamed x1, local copies, waits for them, and re-layouts  2.06 us

profile of v4, /device:TPU:1, one launch (start us, length us, event | category | flops | bytes accessed | tf_op | source)
XLA Modules:
  0.0 87.7 jit_solution(8240160812012065520)
XLA Ops:
  0.0 85.6 %block.1 = bf16[1536,256]{1,0:T(8,128)(2,1)} custom-call(bf16[1536,256]{1,0:T(8,128)(2,1)} %bitcast.10, f32[12,128]{1,0:T(8,128)} %bitcast.13, f32[12,128]{1,0:T(8,128)} %bitcast.14, f32[12,128]{1,0:T(8,128)} %bitcast.15, f32[12,128]{1,0:T(8,128)} %bitcast.16, f32[12,128]{1,0:T(8,128)} %bitcast.17, f32[24,128]{1,0:T(8,128)} %bitcast.12, ...), custom_call_target="tpu_custom_call" | custom-call | tf_op jit(solution)/shard_map/block/pallas_call | solution.py:622
  85.6 2.1 %copy.17 = bf16[1,1536,256]{2,1,0:T(8,128)(2,1)} copy(bf16[1,1536,256]{2,1,0:T(8,128)(2,1)} %bitcast.9) | data formatting | bytes 1572864

commit v5 on v4

--- a/solution.py
+++ b/solution.py
@@ -86,6 +86,23 @@
     return v - jnp.clip(v, -SHRINK, SHRINK)
 
 
+class Several:
+    def __init__(self, copies):
+        self.copies = copies
+
+    def start(self):
+        for copy in self.copies:
+            copy.start()
+
+    def wait_recv(self):
+        for copy in self.copies:
+            copy.wait_recv()
+
+    def wait_send(self):
+        for copy in self.copies:
+            copy.wait_send()
+
+
 def dot_nt(a, b):
     return lax.dot_general(a, b, (((1,), (1,)), ((), ())), preferred_element_type=F32)
 
@@ -107,7 +124,7 @@
     normed, recv1, plane, mid, back, fil, recv2, hid, zt, act, part, precv, own_t,
     w_wide, w_slim, tile, row, mix1, mix2, bias1, bias2, units_bias, fwd, inv,
     s1, r1, s2, r2, loc, zs, zr, ps, pr,
-    zws, zwr, xs, xr, ys, yr, y2s, y2r, ays, ayr, axs, axr, ax2s, ax2r,
+    zws, zwr, xs, xr, ys, yr, y2s, y2r, ays, ayr, axs, axr, ax2s, ax2r, aos, aor, aps, apr,
 ):
     chan = lax.axis_index("chan")
     batch = lax.axis_index("batch")
@@ -158,8 +175,11 @@
             keeps.append(
                 pltpu.make_async_copy(src.at[mine, pl.ds(384 * q, 256)], w_wide.at[ph, q, own_slot], loc.at[ph, q])
             )
-        at = pl.ds(pl.multiple_of(384 * x + 256, 128), 128)
-        keeps.append(pltpu.make_async_copy(src.at[mine, at], w_slim.at[ph, x, own_slot], loc.at[ph, 4]))
+            keeps.append(
+                pltpu.make_async_copy(
+                    src.at[mine, pl.ds(384 * q + 256, 128)], w_slim.at[ph, q, own_slot], loc.at[ph, 4 + q]
+                )
+            )
     for copy in keeps:
         copy.start()
 
@@ -202,10 +222,8 @@
     def write_normed(i, at, v):
         normed[chunk(i), at] = v
 
-    with jax.named_scope("norm1"):
-        norm(load_fields, gain1, shift1, write_normed)
-    with jax.named_scope("greet_wait"):
-        pl.semaphore_wait(barrier, 22)
+    norm(load_fields, gain1, shift1, write_normed)
+    pl.semaphore_wait(barrier, 22)
 
     def to_block(j):
         return remote(
@@ -243,11 +261,21 @@
         return remote(at, at, ays.at[ph, r], ayr.at[ph, r], {1: yp, 2: ym, 3: y2}[r])
 
     def ax(ph, r, way, came):
-        at = group(ph, (x + ((3, 1)[way] if came else 0)) % 4, offs[r])
+        q = (x + ((3, 1)[way] if came else 0)) % 4
+        if r == 0:
+            parts = [(k, w_slim.at[ph, q, slot(0, k)]) for k in (1, 2, 3)]
+            return Several(
+                [remote(at, at, aos.at[ph, way, k], aor.at[ph, way, k], (xp, xm)[way]) for k, at in parts]
+            )
+        at = group(ph, q, offs[r])
         return remote(at, at, axs.at[ph, way, r], axr.at[ph, way, r], (xp, xm)[way])
 
     def ax_pass(ph, r, came):
-        at = group(ph, (x + (2 if came else (3 if r < 2 else 1))) % 4, offs[r])
+        q = (x + (2 if came else (3 if r < 2 else 1))) % 4
+        if r == 0:
+            parts = [(k, w_slim.at[ph, q, slot(0, k)]) for k in (1, 2, 3)]
+            return Several([remote(at, at, aps.at[ph, k], apr.at[ph, k], xp) for k, at in parts])
+        at = group(ph, q, offs[r])
         return remote(at, at, ax2s.at[ph, r], ax2r.at[ph, r], xp if r < 2 else xm)
 
     def start_z(ph):
@@ -261,17 +289,14 @@
 
     for copy in keeps:
         copy.wait()
-    with jax.named_scope("start_z"):
-        start_z(0)
-        start_z(1)
-    with jax.named_scope("blocks_send"):
-        loop(8, lambda i: to_block(15 - i).start())
-    keep = pltpu.make_async_copy(normed.at[rows(chan)], recv1.at[chan, pl.ds(0, CH)], loc.at[0, 5])
+    start_z(0)
+    start_z(1)
+    loop(8, lambda i: to_block(15 - i).start())
+    keep = pltpu.make_async_copy(normed.at[rows(chan)], recv1.at[chan, pl.ds(0, CH)], loc.at[0, 8])
     keep.start()
 
-    with jax.named_scope("start_y"):
-        start_y(0, 0)
-        start_y(1, 0)
+    start_y(0, 0)
+    start_y(1, 0)
     loop(7, lambda i: to_block(7 - i).start())
 
     def service_z(ph):
@@ -307,10 +332,9 @@
             ax(ph, r, 0 if r < 2 else 1, True).wait_recv()
             ax_pass(ph, r, False).start()
 
-    with jax.named_scope("service_1"):
-        service_z(0)
-        service_y(0, (0,))
-        service_z(1)
+    service_z(0)
+    service_y(0, (0,))
+    service_z(1)
     tile[...] = jnp.zeros_like(tile)
     row[...] = jnp.zeros_like(row)
 
@@ -353,18 +377,15 @@
         recv1[a, pl.ds(CH, 32), :] = jnp.zeros((32, TOK), BF16)
         back[a, :, pl.ds(128, 128)] = jnp.zeros((2 * CH, 128), F32)
 
-    with jax.named_scope("clear"):
-        loop(16, clear)
+    loop(16, clear)
 
     keep.wait()
-    with jax.named_scope("service_2"):
-        service_x(0)
-        service_a(0)
-        service_y(1, (0,))
-
-    with jax.named_scope("service_3"):
-        service_x(1)
-        service_y(0, (1,))
+    service_x(0)
+    service_a(0)
+    service_y(1, (0,))
+
+    service_x(1)
+    service_y(0, (1,))
 
     def planes(p):
         both = recv1[pl.ds(2 * p, 2)].reshape(256, TOK)
@@ -375,10 +396,9 @@
         from_plane(2 * i + 1).wait_recv()
         planes(peer(2 * i, -1) // 2)
 
-    with jax.named_scope("planes"):
-        from_plane(1).wait_recv()
-        planes(chan // 2)
-        loop(8, planes_in, start=1)
+    from_plane(1).wait_recv()
+    planes(chan // 2)
+    loop(8, planes_in, start=1)
 
 
     def lines(t):
@@ -393,8 +413,7 @@
             plane[a // 2, re_at, lanes] = re
             plane[a // 2, im_at, lanes] = im
 
-    with jax.named_scope("lines"):
-        loop(18, lines, unroll=2)
+    loop(18, lines, unroll=2)
 
     def mix_in(p):
         v = plane[p].astype(BF16)
@@ -412,12 +431,10 @@
             res = dot_nt(mix2[...], mid[p, pl.ds(half * MODES, MODES), :]) + bias2[...]
             back[2 * p + half, :, pl.ds(0, MODES)] = shrink(res)
 
-    with jax.named_scope("mix"):
-        loop(8, mix_in, unroll=2)
-        loop(8, mix_out, unroll=2)
-    with jax.named_scope("service_4"):
-        service_y(0, (2, 3))
-        service_a(1)
+    loop(8, mix_in, unroll=2)
+    loop(8, mix_out, unroll=2)
+    service_y(0, (2, 3))
+    service_a(1)
 
     def lines_back(t):
         re_at = pl.ds(pl.multiple_of((t // 2) * 8, 8), 8)
@@ -428,8 +445,7 @@
             back[a, re_at, lanes] = re
             back[a, im_at, lanes] = im
 
-    with jax.named_scope("lines_back"):
-        loop(24, lines_back, unroll=2)
+    loop(24, lines_back, unroll=2)
 
     def planes_back(p):
         lhs = [
@@ -452,17 +468,15 @@
         to_plane(14 - 2 * i).start()
         to_plane(15 - 2 * i).start()
 
-    with jax.named_scope("planes_back"):
-        loop(7, planes_out)
-        planes_back(chan // 2)
+    loop(7, planes_out)
+    planes_back(chan // 2)
     to_plane(1).start()
-    keep = pltpu.make_async_copy(fil.at[chan], recv2.at[rows(chan)], loc.at[1, 5])
+    keep = pltpu.make_async_copy(fil.at[chan], recv2.at[rows(chan)], loc.at[1, 8])
     keep.start()
-    with jax.named_scope("service_5"):
-        service_y(1, (1,))
-        service_ax(0)
-        service_y(1, (2, 3))
-        service_ax(1)
+    service_y(1, (1,))
+    service_ax(0)
+    service_y(1, (2, 3))
+    service_ax(1)
     keep.wait()
 
     def take(p, acc):
@@ -474,8 +488,7 @@
         from_block(j).wait_recv()
         return take(peer(j, -1), acc)
 
-    with jax.named_scope("filtered_wait"):
-        channel_sum = lax.fori_loop(1, 16, take_next, take(chan, jnp.zeros((8, TOK), F32)))
+    channel_sum = lax.fori_loop(1, 16, take_next, take(chan, jnp.zeros((8, TOK), F32)))
 
     def write_z(i, at, v):
         recv2[chunk(i), at] = v
@@ -483,8 +496,7 @@
     def load_hidden(i):
         return hid[chunk(i), :]
 
-    with jax.named_scope("norm2"):
-        norm(load_hidden, gain2, shift2, write_z, channel_sum)
+    norm(load_hidden, gain2, shift2, write_z, channel_sum)
 
     eye = (
         lax.broadcasted_iota(jnp.int32, (TOK, TOK), 0) == lax.broadcasted_iota(jnp.int32, (TOK, TOK), 1)
@@ -494,8 +506,7 @@
         at = pl.ds(pl.multiple_of(i * 256, 256), 256)
         zt[0, :, at] = dot_nt(eye, recv2[at, :]).astype(BF16)
 
-    with jax.named_scope("turn"):
-        loop(6, turn)
+    loop(6, turn)
     send_z = remote(zt.at[0], zt.at[1], zs, zr, mate)
     send_z.start()
 
@@ -524,28 +535,21 @@
         for k in range(4):
             y_pass(ph, k, True).wait_recv()
 
-    with jax.named_scope("win_wait"):
-        for k in (2, 3):
-            y_move(0, k, 0, True).wait_recv()
-        for r in range(4):
-            ax(0, r, 0 if r >= 2 else 1, True).wait_recv()
-        for k in range(4):
-            ax_pass(0, k, True).wait_recv()
-    with jax.named_scope("units_own_a"):
-        units(0, 0)
-    with jax.named_scope("win_wait_b"):
-        for k in (0, 1):
-            y_move(0, k, 1, True).wait_recv()
-        for k in range(4):
-            y_pass(0, k, True).wait_recv()
-    with jax.named_scope("units_own_b"):
-        units(1, 0)
-    with jax.named_scope("z_wait"):
-        send_z.wait_recv()
-    with jax.named_scope("units_mate"):
-        [units(i, 1) for i in range(2)]
-    with jax.named_scope("wout_wait"):
-        arrived(1)
+    for k in (2, 3):
+        y_move(0, k, 0, True).wait_recv()
+    for r in range(4):
+        ax(0, r, 0 if r >= 2 else 1, True).wait_recv()
+    for k in range(4):
+        ax_pass(0, k, True).wait_recv()
+    units(0, 0)
+    for k in (0, 1):
+        y_move(0, k, 1, True).wait_recv()
+    for k in range(4):
+        y_pass(0, k, True).wait_recv()
+    units(1, 0)
+    send_z.wait_recv()
+    [units(i, 1) for i in range(2)]
+    arrived(1)
 
     def project(t, write):
         def wide(q):
@@ -566,15 +570,12 @@
     def write_own(at, v):
         own_t[:, at] = v
 
-    with jax.named_scope("project_mate"):
-        project(1, write_part)
+    project(1, write_part)
     send_part = remote(part, precv, ps, pr, mate)
     send_part.start()
 
-    with jax.named_scope("project_own"):
-        project(0, write_own)
-    with jax.named_scope("part_wait"):
-        send_part.wait_recv()
+    project(0, write_own)
+    send_part.wait_recv()
 
     def finish(i):
         at = pl.ds(pl.multiple_of(i * 128, 128), 128)
@@ -583,8 +584,7 @@
         for to in (slice(0, 128), slice(128, 256)):
             out[at, to] = (hid[at, to] + total[:, to] + shift).astype(BF16)
 
-    with jax.named_scope("finish"):
-        loop(12, finish)
+    loop(12, finish)
 
     loop(15, lambda i: to_block(15 - i).wait_send())
     loop(15, lambda i: to_plane(15 - i).wait_send())
@@ -604,9 +604,8 @@
             y_pass(ph, k, False).wait_send()
             ax_pass(ph, k, False).wait_send()
 
-    with jax.named_scope("sent"):
-        sent(0)
-        sent(1)
+    sent(0)
+    sent(1)
 
 
 def on_device(
@@ -649,11 +648,11 @@
             pltpu.VMEM((4, 8, 384), F32),
             pltpu.VMEM((2 * MODES, TOK), BF16),
             pltpu.VMEM((512, TOK), BF16),
-            dma((16,)), dma((16,)), dma((16,)), dma((16,)), dma((2, 6)),
+            dma((16,)), dma((16,)), dma((16,)), dma((16,)), dma((2, 9)),
             dma, dma, dma, dma,
             dma((2, 2, 4)), dma((2, 2, 4)), dma((2, 3, 4)), dma((2, 3, 4)), dma((2, 2, 4)), dma((2, 2, 4)),
             dma((2, 4)), dma((2, 4)), dma((2, 4)), dma((2, 4)), dma((2, 2, 4)), dma((2, 2, 4)),
-            dma((2, 4)), dma((2, 4)),
+            dma((2, 4)), dma((2, 4)), dma((2, 2, 4)), dma((2, 2, 4)), dma((2, 4)), dma((2, 4)),
         ],
         compiler_params=pltpu.CompilerParams(
             collective_id=0, has_side_effects=True, vmem_limit_bytes=56 * 2**20

time: 89.3 us -> 89.1 us (level)
  no operation moved by 1% of the time
where the time goes in v5:
time: 89.1 us; the launch traced here: 88.2 us
  Pallas kernels  86.1 us (97%)
  local copies, waits for them, and re-layouts  2.06 us (2%)
    pallas_call x1, Pallas kernels, on_device(): pl.pallas_call(kernel, out_shape=jax.ShapeDtypeStruct((D, TOK), BF16), in...  86.1 us
    unnamed x1, local copies, waits for them, and re-layouts  2.06 us

profile of v5, /device:TPU:1, one launch (start us, length us, event | category | flops | bytes accessed | tf_op | source)
XLA Modules:
  0.0 88.2 jit_solution(4133666393474092355)
XLA Ops:
  0.0 86.1 %block.1 = bf16[1536,256]{1,0:T(8,128)(2,1)} custom-call(bf16[1536,256]{1,0:T(8,128)(2,1)} %bitcast.10, f32[12,128]{1,0:T(8,128)} %bitcast.13, f32[12,128]{1,0:T(8,128)} %bitcast.14, f32[12,128]{1,0:T(8,128)} %bitcast.15, f32[12,128]{1,0:T(8,128)} %bitcast.16, f32[12,128]{1,0:T(8,128)} %bitcast.17, f32[24,128]{1,0:T(8,128)} %bitcast.12, ...), custom_call_target="tpu_custom_call" | custom-call | tf_op jit(solution)/shard_map/block/pallas_call | solution.py:621
  86.1 2.1 %copy.17 = bf16[1,1536,256]{2,1,0:T(8,128)(2,1)} copy(bf16[1,1536,256]{2,1,0:T(8,128)(2,1)} %bitcast.9) | data formatting | bytes 1572864
